TPU v7x, 128 devices: a whole 4x4x4 slice. The times are simulated.
128 devices in a mesh: blk: 8 (over x, core), line: 16 (over z, y).
Axes of the slice: x: 4, y: 4, z: 4, core: 2. Of those that a mesh axis runs over, the one named last changes fastest.
Arguments:
- state: float32 [8, 5, 256, 64, 128], P('blk', None, None, 'line'), may hold values from -6 to 6
- first_flux: float32 [8, 5, 5], P('blk'), may hold values from -1.25 to 1.25
- second_flux: float32 [8, 5, 5], P('blk'), may hold values from -1.25 to 1.25
- viscosity: float32 [8], P('blk'), may hold values from 0.02 to 0.15
- first_inverse: float32 [8, 256, 256], P('blk'), may hold values from 0 to 1.7
- second_inverse: float32 [8, 64, 64], P('blk'), may hold values from 0 to 1.7
- donor_cell: int32 [128, 128, 128], P(('blk', 'line')), may hold values from 0 to 131070, as said below
- donor_weight: float32 [128, 128, 128], P(('blk', 'line')), may hold values from 0 to 1
- receptor_cell: int32 [128, 128, 128], P(('blk', 'line')), may hold values from 0 to 131072, as said below
Outputs:
- advanced: float32 [8, 5, 256, 64, 128], P('blk', None, None, 'line')
Inputs may be any that keep to these rules, and one draw needn't show every extreme that they name: `donor_cell`: entry [n, m, p] is a local cell index of sending piece n whose third-direction index is below 127. `receptor_cell`: entry [m, n, p] is the local cell of receiving piece m that takes slot p from sending piece n, or 131072 where the slot is unused; the used cells of one receiving piece are distinct; pieces of the same block exchange nothing; every receiving piece has one sending piece whose 128 slots are all used.
All inputs are finite; a program needn't handle non-finite values.
Results may differ from a plain program's by a relative error of at most 0.0003.
Values sent between devices are 32-bit elements; how exact they have to be, the bound alone decides.
No kernel may reach another device: no remote copies, remote signals or barrier semaphores. Data moves between devices by JAX's collectives and lax.ppermute only.
A program may use at most 256 MiB of HBM per device.

v0:
```python
import jax
import jax.numpy as jnp
from jax import lax
from jax.sharding import PartitionSpec as P

highest = lax.Precision.HIGHEST


def padded_2(cells, sides, width):
    for axis, dim in sides:
        count = lax.axis_size(axis)
        ends = count - 1
        head = lax.slice_in_dim(cells, 0, width, axis=dim)
        tail = lax.slice_in_dim(cells, cells.shape[dim] - width, cells.shape[dim], axis=dim)
        cells = jnp.concatenate(
            [
                lax.ppermute(tail, axis, [(i, (i + 1) % count) for i in range(ends)]),
                cells,
                lax.ppermute(head, axis, [((i + 1) % count, i) for i in range(ends)]),
            ],
            axis=dim,
        )
    return cells


def explicit_rhs(padded, field, across_flux, lateral_flux, damping):
    plus_i = padded[:, 2:, 1:-1, 1:-1]
    minus_i = padded[:, :-2, 1:-1, 1:-1]
    plus_j = padded[:, 1:-1, 2:, 1:-1]
    minus_j = padded[:, 1:-1, :-2, 1:-1]
    plus_k = padded[:, 1:-1, 1:-1, 2:]
    minus_k = padded[:, 1:-1, 1:-1, :-2]
    laplace = plus_i + minus_i + plus_j + minus_j + plus_k + minus_k - 6.0 * field
    convect = jnp.einsum("uv,vijk->uijk", across_flux, plus_i - minus_i, precision=highest)
    convect = convect + jnp.einsum(
        "uv,vijk->uijk", lateral_flux, plus_j - minus_j, precision=highest
    )
    return damping * laplace - 0.5 * convect


def body(
    state,
    first_flux,
    second_flux,
    viscosity,
    first_inverse,
    second_inverse,
    donor_cell,
    donor_weight,
    receptor_cell,
):
    blocks_here = lax.axis_size("blk")
    ranges_here = lax.axis_size("line")
    pieces_here = blocks_here * ranges_here
    field = state[0]
    variables, rows_i, cols_j, depth = field.shape
    total = rows_i * cols_j * depth
    slot_count = donor_cell.shape[2]
    cells_out = donor_cell[0].reshape(-1)
    weights = donor_weight[0].reshape(-1)
    cells_in = receptor_cell[0].reshape(-1)
    across_flux = first_flux[0]
    lateral_flux = second_flux[0]
    damping = viscosity[0]
    inverse_i = first_inverse[0]
    inverse_j = second_inverse[0]
    local = field.reshape(variables, total)
    first_value = jnp.take(local, cells_out, axis=1)
    second_value = jnp.take(local, cells_out + 1, axis=1)
    donated = (weights * first_value + (1.0 - weights) * second_value).reshape(
        variables, pieces_here, slot_count
    )
    arrived = lax.all_to_all(donated, ("blk", "line"), split_axis=1, concat_axis=1, tiled=True)
    fringed = local.at[:, cells_in].set(arrived.reshape(variables, -1), mode="drop")
    fringed = fringed.reshape(variables, rows_i, cols_j, depth)
    rimmed = padded_2(fringed, (("line", 2),), 1)
    padded = jnp.pad(rimmed, ((0, 0), (1, 1), (0, 0), (1, 1)))
    rhs_part = explicit_rhs(padded, fringed, across_flux, lateral_flux, damping)
    line_i = jnp.einsum("ab,vbjk->vajk", inverse_i, rhs_part, precision=highest)
    product = jnp.einsum(
        "ab,vibk->viak",
        inverse_j,
        lax.all_to_all(line_i, "line", split_axis=1, concat_axis=2, tiled=True),
        precision=highest,
    )
    line_j = lax.all_to_all(product, "line", split_axis=2, concat_axis=1, tiled=True)
    field = fringed + line_j
    return field[None]


def solution(mesh):
    in_specs = (
        P("blk", None, None, "line", None),
        P("blk", None, None),
        P("blk", None, None),
        P("blk"),
        P("blk", None, None),
        P("blk", None, None),
        P(("blk", "line"), None, None),
        P(("blk", "line"), None, None),
        P(("blk", "line"), None, None),
    )
    out_specs = P("blk", None, None, "line", None)
    return jax.shard_map(body, mesh=mesh, in_specs=in_specs, out_specs=out_specs, check_vma=False)
```

profile of v0, /device:TPU:0, one launch (start us, length us, event | category | flops | bytes accessed | tf_op | source)
XLA Modules:
  0.0 961.2 jit_solution(1174983305058571013)
XLA Ops:
  0.0 0.0 copy-start
  0.0 0.9 fusion.26
  0.9 0.9 compare_and_fusion.1
  1.8 30.6 %copy.57 = f32[1,5,256,4,128]{1,4,3,2,0:T(8,128)} copy(f32[1,5,256,4,128]{4,3,2,1,0:T(4,128)} %param.11) | data formatting | bytes 5242880 | tf_op args[0]
  32.4 0.0 copy-start.2
  32.4 236.2 %gather_fusion = f32[16384,5]{1,0:T(8,128)} fusion(f32[5,131072]{0,1:T(8,128)} %bitcast, s32[16384]{0:T(1024)S(1)} %get-tuple-element.12), kind=kCustom, calls=%fused_computation.clone | custom fusion | bytes 720896 | tf_op jit(solution)/shard_map/jit(_take)/gather | solution.py:68
  268.6 236.3 %gather_fusion.1 = f32[16384,5]{1,0:T(8,128)} fusion(f32[5,131072]{0,1:T(8,128)} %bitcast, s32[16384]{0:T(1024)S(1)} %get-tuple-element.13), kind=kCustom, calls=%fused_computation.1.clone | custom fusion | bytes 720896 | tf_op jit(solution)/shard_map/jit(_take)/gather | solution.py:69
  504.9 0.0 copy-done.2
  504.9 17.1 %fusion.8 = f32[5,16384]{0,1:T(8,128)} fusion(f32[16384,5]{1,0:T(8,128)} %gather_fusion.1, f32[16384,5]{1,0:T(8,128)} %gather_fusion, f32[16384]{0:T(1024)S(1)} %broadcast_subtract_fusion, f32[16384]{0:T(1024)S(1)} %bitcast.83, pred[16384]{0:T(1024)(128)(4,1)S(1)} %get-tuple-element.11, pred[16384]{0:T(1024)(128)(4,1)S(1)} %get-tuple-element.10), kind=kLoop, calls=%fused_computation.16 | loop fusion | flops 409600 | bytes 1146880 | tf_op jit(solution)/shard_map/add | solution.py:70
  522.1 0.0 copy-start.3
  522.1 6.1 copy.58
  528.1 11.8 %all-to-all-start = ((f32[5,128,128]{2,0,1:T(8,128)}), f32[5,128,128]{2,0,1:T(8,128)S(1)}, u32[]{:S(2)}, u32[]{:S(2)}) async-start(f32[5,128,128]{2,0,1:T(8,128)} %copy.58), calls=%async_computation | async-start | bytes 1048576 | tf_op jit(solution)/shard_map/all_to_all | solution.py:73
  540.0 0.0 copy-done.3
  540.0 0.1 compare_select_fusion
  540.1 7.1 sort
  547.3 6.3 all-to-all-done
  553.6 5.2 copy.59
  558.8 178.3 %scatter_custom_fusion = f32[5,131072]{0,1:T(8,128)} fusion(f32[5,131072]{0,1:T(8,128)} %bitcast, s32[16384]{0:T(1024)S(1)} %get-tuple-element.6, f32[16384,5]{1,0:T(8,128)} %copy.59, s32[16384]{0:T(1024)S(1)} %broadcast_clamp_fusion), kind=kCustom, calls=%fused_computation.13 | custom fusion | bytes 2621440 | tf_op jit(solution)/shard_map/scatter | solution.py:74
  737.1 21.3 %fusion.34 = (f32[5,256,1,128]{0,3,2,1:T(8,128)}, f32[5,256,1,128]{0,3,2,1:T(8,128)}) fusion(f32[5,256,4,128]{0,3,2,1:T(8,128)} %bitcast.12), kind=kLoop, calls=%fused_computation.52 | loop fusion | bytes 2621440 | tf_op jit(solution)/shard_map/slice | solution.py:14
  758.5 10.0 %copy.89 = f32[5,256,1,128]{3,2,1,0:T(1,128)S(1)} copy(f32[5,256,1,128]{0,3,2,1:T(8,128)} %get-tuple-element.8) | data formatting | bytes 1310720
  768.5 2.6 collective-permute-start
  771.1 10.0 %copy.90 = f32[5,256,1,128]{3,2,1,0:T(1,128)S(1)} copy(f32[5,256,1,128]{0,3,2,1:T(8,128)} %get-tuple-element.9) | data formatting | bytes 1310720
  781.2 1.8 collective-permute-start.1
  783.6 35.7 %copy.64 = f32[5,256,4,128]{3,0,2,1:T(8,128)} copy(f32[5,256,4,128]{0,3,2,1:T(8,128)} %bitcast.12) | data formatting | bytes 5242880 | tf_op jit(solution)/shard_map/reshape | solution.py:75
  819.4 0.0 collective-permute-done
  819.4 0.4 copy.63
  819.8 0.0 collective-permute-done.1
  819.8 0.4 copy.65
  820.2 0.0 copy-start.1
  820.2 0.0 copy-start.5
  820.2 10.7 %select_maximum_fusion = f32[5,258,6,130]{3,0,2,1:T(8,128)} fusion(f32[5,256,1,128]{3,0,2,1:T(8,128)S(1)} %copy.65, f32[5,256,4,128]{3,0,2,1:T(8,128)} %copy.64, f32[5,256,1,128]{3,0,2,1:T(8,128)S(1)} %copy.63), kind=kLoop, calls=%fused_computation.8 | loop fusion | flops 15093000 | bytes 7956960 | tf_op jit(solution)/shard_map/concatenate | solution.py:15
  830.9 0.0 copy-done.1
  830.9 0.0 copy-done.5
  831.0 0.0 copy-start.6
  831.0 5.6 fusion.12
  836.5 0.0 copy-done.6
  836.5 20.7 %fusion.11 = f32[5,256,4,128]{3,0,2,1:T(8,128)} fusion(f32[5,258,6,130]{3,0,2,1:T(8,128)} %select_maximum_fusion, f32[256,4,128,5]{2,3,1,0:T(8,128)} %fusion.12, f32[5,256,4,128]{3,0,2,1:T(8,128)S(1)} %copy-done.1, f32[5,256,1,128]{3,0,2,1:T(8,128)S(1)} %copy.65, f32[5,256,1,128]{3,0,2,1:T(8,128)S(1)} %copy.63, f32[]{:T(128)} %bitcast.75, ...), kind=kOutput, calls=%fused_computation.21 | convolution fusion | flops 48496640 | bytes 35914340 | tf_op jit(solution)/shard_map/uv,vijk->uijk/dot_general | solution.py:34
  857.3 0.0 copy-done
  857.3 7.4 fusion.22
  864.7 2.6 copy.72
  867.3 40.2 %all_to_all.41 = f32[5,256,4,128]{3,2,0,1:T(4,128)S(1)} all-to-all(f32[5,256,4,128]{3,2,0,1:T(4,128)} %copy.72), channel_id=1, replica_groups=mesh['blk'=8,'line'=16] {'line'}, dimensions={1} | all-to-all | bytes 5242880 | tf_op jit(solution)/shard_map/all_to_all | solution.py:83
  907.5 0.0 copy-start.4
  907.5 0.3 copy.73
  907.8 1.7 copy.74
  909.5 0.0 copy-done.4
  909.5 2.6 convolution_bitcast_fusion
  912.1 3.0 copy.75
  915.1 4.7 all-to-all-start.2
  919.8 34.5 %copy.77 = f32[1,5,256,4,128]{4,3,2,1,0:T(4,128)S(1)} copy(f32[1,5,256,4,128]{1,4,3,2,0:T(8,128)} %bitcast.10) | data formatting | bytes 5242880 | tf_op jit(solution)/shard_map/reshape | solution.py:75
  954.3 1.5 all-to-all-done.2
  955.8 3.0 copy.76
  958.8 2.2 add.70
  (3 shorter events, 0.0 us)
Async XLA Ops:
  0.0 857.3 %copy-start = (f32[1,256,256]{2,1,0:T(8,128)S(1)}, f32[1,256,256]{2,1,0:T(8,128)}, u32[]{:S(2)}) copy-start(f32[1,256,256]{2,1,0:T(8,128)} %param.15) | copy-start | bytes 786436
  32.4 472.5 %copy-start.2 = (f32[1,128,128]{2,1,0:T(8,128)S(1)}, f32[1,128,128]{2,1,0:T(8,128)}, u32[]{:S(2)}) copy-start(f32[1,128,128]{2,1,0:T(8,128)} %param.18) | copy-start | bytes 196612
  522.1 17.9 %copy-start.3 = (s32[1,128,128]{2,1,0:T(8,128)S(1)}, s32[1,128,128]{2,1,0:T(8,128)}, u32[]{:S(2)}) copy-start(s32[1,128,128]{2,1,0:T(8,128)} %param.19) | copy-start | bytes 196612
  528.1 25.4 %all-to-all-start = ((f32[5,128,128]{2,0,1:T(8,128)}), f32[5,128,128]{2,0,1:T(8,128)S(1)}, u32[]{:S(2)}, u32[]{:S(2)}) async-start(f32[5,128,128]{2,0,1:T(8,128)} %copy.58), calls=%async_computation | async-start | bytes 1048576 | tf_op jit(solution)/shard_map/all_to_all | solution.py:73
  768.5 50.9 %collective-permute-start = (f32[5,256,1,128]{3,1,2,0:T(8,128)S(1)}, f32[5,256,1,128]{3,1,2,0:T(8,128)S(1)}, u32[]{:S(2)}, u32[]{:S(2)}) collective-permute-start(f32[5,256,1,128]{3,1,2,0:T(8,128)S(1)} %bitcast.81), channel_id=1, source_target_pairs={{0,1},{1,2},{2,3},{3,4},{4,5},{5,6},{6,7},{7,8},{8,9},{9,10},{10,1... | collective-permute-start | bytes 1966088 | tf_op jit(solution)/shard_map/ppermute | solution.py:17
  781.2 38.6 %collective-permute-start.1 = (f32[5,256,1,128]{3,1,2,0:T(8,128)S(1)}, f32[5,256,1,128]{3,1,2,0:T(8,128)S(1)}, u32[]{:S(2)}, u32[]{:S(2)}) collective-permute-start(f32[5,256,1,128]{3,1,2,0:T(8,128)S(1)} %bitcast.82), channel_id=1, source_target_pairs={{1,0},{2,1},{3,2},{4,3},{5,4},{6,5},{7,6},{8,7},{9,8},{10,9},{11,1... | collective-permute-start | bytes 1966088 | tf_op jit(solution)/shard_map/ppermute | solution.py:19
  820.2 10.8 %copy-start.1 = (f32[5,256,4,128]{3,0,2,1:T(8,128)S(1)}, f32[5,256,4,128]{3,0,2,1:T(8,128)}, u32[]{:S(2)}) copy-start(f32[5,256,4,128]{3,0,2,1:T(8,128)} %copy.64) | copy-start | bytes 7864324
  820.2 10.7 %copy-start.5 = (f32[1,5,5]{2,0,1:T(1,128)S(1)}, f32[1,5,5]{2,0,1:T(1,128)}, u32[]{:S(2)}) copy-start(f32[1,5,5]{2,0,1:T(1,128)} %param.13) | copy-start | bytes 304
  831.0 5.6 copy-start.6
  907.5 2.0 copy-start.4
  915.1 40.7 %all-to-all-start.2 = ((f32[5,16,64,128]{3,1,0,2:T(8,128)}), f32[5,16,64,128]{3,1,0,2:T(8,128)}, u32[]{:S(2)}, u32[]{:S(2)}) async-start(f32[5,16,64,128]{3,1,0,2:T(8,128)} %copy.75), calls=%async_computation.2 | async-start | bytes 5242880 | tf_op jit(solution)/shard_map/all_to_all | solution.py:86
where the time goes:
time: 970 us; the launch traced here: 961 us
  local copies, waits for them, and re-layouts  816 us (84%)
  blocking collectives  40.2 us (4%)
  other arithmetic  39.1 us (4%)
  matrix products  36.3 us (4%)
  starting transfers between devices  20.9 us (2%)
    gather x1, local copies, waits for them, and re-layouts, body(): second_value = jnp.take(local, cells_out + 1, axis=1)  236 us
    gather x1, local copies, waits for them, and re-layouts, body(): first_value = jnp.take(local, cells_out, axis=1)  236 us
    scatter x2, local copies, waits for them, and re-layouts, body(): local.at[:, cells_in].set(arrived.reshape(variables, -1), mode='drop')  178 us
    reshape x2, local copies, waits for them, and re-layouts, body(): fringed = fringed.reshape(variables, rows_i, cols_j, depth)  70.2 us
    unnamed x17, local copies, waits for them, and re-layouts  50.7 us
    all_to_all x1, blocking collectives, body(): lax.all_to_all(line_i, 'line', split_axis=1, concat_axis=2, tiled=True)  40.2 us
    slice x1, local copies, waits for them, and re-layouts, padded_2(): lax.slice_in_dim(cells, cells.shape[dim] - width, cells.shape[dim], axis=...  21.3 us
    dot_general x1, matrix products, explicit_rhs(): jnp.einsum('uv,vijk->uijk', across_flux, plus_i - minus_i, precision=high...  20.7 us
  transfers between devices with their start and end apart: 4, of which 2 were waited for; matrix products, arithmetic and copies ran while one was open for 9% of the time, Pallas kernels for 0%

commit v1 on v0

v1 whole, which is shorter than its diff:
```python
import jax
import jax.numpy as jnp
from jax import lax
from jax.experimental import pallas as pl
from jax.experimental.pallas import tpu as pltpu
from jax.sharding import PartitionSpec as P

V, NI, CJ, NK, PIECES, SLOTS, RANGES = 5, 256, 4, 128, 128, 128, 16
ROWS = NI * CJ
CHUNK = NI // RANGES
NJ = CJ * RANGES
highest = lax.Precision.HIGHEST
f32 = jnp.float32


def to_rows(st_ref, tiles):
    def one(b, carry):
        for v in range(V):
            tiles[pl.ds(b * 64 + v, 8, stride=8), :] = st_ref[pl.ds(v * ROWS + b * 8, 8), :]
        return carry

    lax.fori_loop(0, ROWS // 8, one, 0)


def tile_of(tiles, cell):
    return tiles.at[pl.ds(pl.multiple_of((cell >> 7) * 8, 8), 8), :]


def gather_kernel(cell_ref, lane_ref, weight_ref, st_ref, out_ref, tiles):
    to_rows(st_ref, tiles)
    lane = lax.broadcasted_iota(jnp.int32, (8, 128), 1)
    odd = lane & 1
    half = lane >> 1
    even = (lane * 2) & 127

    def piece(m, carry):
        cells = jnp.broadcast_to(lane_ref[pl.ds(m, 1), :] & 127, (8, 128))
        weights = jnp.broadcast_to(weight_ref[pl.ds(m, 1), :], (8, 128))
        sums = []
        for h in range(2):
            pick = half + 64 * h
            want = jnp.take_along_axis(cells, pick, axis=1) + odd
            w = jnp.take_along_axis(weights, pick, axis=1)
            w = jnp.where(odd == 0, w, 1.0 - w)
            acc = jnp.zeros((8, 128), f32)
            for q in range(64):
                x = tile_of(tiles, cell_ref[m, 64 * h + q])[...]
                acc = jnp.where(half == q, jnp.take_along_axis(x, want, axis=1), acc)
            acc = acc * w
            acc = acc + pltpu.roll(acc, 127, axis=1)
            sums.append(jnp.take_along_axis(acc, even, axis=1))
        out_ref[m] = jnp.where(lane < 64, sums[0], sums[1])[:V]
        return carry

    lax.fori_loop(0, PIECES, piece, 0)


def scatter_kernel(cell_ref, arrived_ref, st_ref, field_ref, edge_ref, tiles):
    to_rows(st_ref, tiles)
    lane = lax.broadcasted_iota(jnp.int32, (8, 128), 1)

    def piece(n, carry):
        values = jnp.concatenate([arrived_ref[n], jnp.zeros((3, 128), f32)], axis=0)
        for p in range(SLOTS):
            cell = cell_ref[n, p]
            value = jnp.broadcast_to(values[:, p : p + 1], (8, 128))
            pltpu.store(tile_of(tiles, cell), value, mask=lane == (cell & 127))
        return carry

    lax.fori_loop(0, PIECES, piece, 0)
    zero = jnp.zeros((8, 128), f32)
    for j in range(CJ):
        for v in range(V):
            field_ref[j, v, pl.ds(0, 8), :] = zero
            field_ref[j, v, pl.ds(NI + 8, 8), :] = zero

    def one(b, carry):
        for j in range(CJ):
            for v in range(V):
                x = tiles[pl.ds(b * 256 + j * 8 + v, 8, stride=32), :]
                field_ref[j, v, pl.ds(8 + b * 8, 8), :] = x
                if j in (0, CJ - 1):
                    edge_ref[j // (CJ - 1), v, pl.ds(b * 8, 8), :] = x
        return carry

    lax.fori_loop(0, NI // 8, one, 0)


def first_kernel(js, a_ref, b_ref, damp_ref, field_ref, low_ref, high_ref, inverse_ref, out_ref, rhs):
    lane = lax.broadcasted_iota(jnp.int32, (8, 128), 1)
    damp = damp_ref[0]
    a = [[0.5 * a_ref[0, u, v] for v in range(V)] for u in range(V)]
    b = [[0.5 * b_ref[0, u, v] for v in range(V)] for u in range(V)]
    for slot, j in enumerate(js):

        def one(t, carry):
            base = pl.multiple_of(t * 8, 8)
            di, dj, lap = [], [], []
            for v in range(V):
                c = field_ref[j, v, pl.ds(base + 8, 8), :]
                wide = field_ref[j, v, pl.ds(base, 24), :]
                im, ip = wide[7:15], wide[9:17]
                if j == 0:
                    jm = low_ref[v, pl.ds(base, 8), :]
                else:
                    jm = field_ref[j - 1, v, pl.ds(base + 8, 8), :]
                if j == CJ - 1:
                    jp = high_ref[v, pl.ds(base, 8), :]
                else:
                    jp = field_ref[j + 1, v, pl.ds(base + 8, 8), :]
                kp = jnp.where(lane == NK - 1, 0.0, pltpu.roll(c, NK - 1, axis=1))
                km = jnp.where(lane == 0, 0.0, pltpu.roll(c, 1, axis=1))
                lap.append(ip + im + jp + jm + kp + km - 6.0 * c)
                di.append(ip - im)
                dj.append(jp - jm)
            for u in range(V):
                r = damp * lap[u]
                for v in range(V):
                    r = r - (a[u][v] * di[v] + b[u][v] * dj[v])
                rhs[pl.ds(base, 8), pl.ds(u * NK, NK)] = r
            return carry

        lax.fori_loop(0, NI // 8, one, 0)
        solved = jnp.dot(inverse_ref[...], rhs[...], precision=highest, preferred_element_type=f32)
        for u in range(V):
            out_ref[:, u, slot] = solved[:, u * NK : (u + 1) * NK].reshape(RANGES, CHUNK, NK)


def second_kernel(inverse_ref, in_ref, out_ref, wide, solved):
    step = V * CJ * CHUNK
    for v in range(V):
        for j in range(CJ):
            for i in range(CHUNK):
                for s in range(0, RANGES, 8):
                    start = s * step + (v * CJ + j) * CHUNK + i
                    wide[j * RANGES + s : j * RANGES + s + 8, i * NK : (i + 1) * NK] = in_ref[
                        pl.ds(start, 8, stride=step), :
                    ]
        solved[...] = jnp.dot(inverse_ref[...], wide[...], precision=highest, preferred_element_type=f32)
        for j in range(CJ):
            for i in range(CHUNK):
                for s in range(0, RANGES, 8):
                    start = s * step + (v * CJ + j) * CHUNK + i
                    out_ref[pl.ds(start, 8, stride=step), :] = solved[
                        j * RANGES + s : j * RANGES + s + 8, i * NK : (i + 1) * NK
                    ]


def add_kernel(field_ref, back_ref, out_ref):
    def one(t, carry):
        for v in range(V):
            for j in range(CJ):
                for h in range(CHUNK // 8):
                    i = t * CHUNK + h * 8
                    x = field_ref[j, v, pl.ds(pl.multiple_of(i + 8, 8), 8), :] + back_ref[t, v, j, pl.ds(h * 8, 8), :]
                    out_ref[pl.ds(v * ROWS + i * CJ + j, 8, stride=CJ), :] = x
        return carry

    lax.fori_loop(0, RANGES, one, 0)


smem = pl.BlockSpec(memory_space=pltpu.SMEM)
vmem = pl.BlockSpec(memory_space=pltpu.VMEM)


def run(kernel, specs, shapes, scratch, limit, *args):
    one = not isinstance(shapes, list)
    shapes = [shapes] if one else shapes
    out = pl.pallas_call(
        kernel,
        out_shape=[jax.ShapeDtypeStruct(s, f32) for s in shapes],
        in_specs=specs,
        out_specs=[vmem] * len(shapes),
        scratch_shapes=[pltpu.VMEM(s, f32) for s in scratch],
        compiler_params=pltpu.CompilerParams(vmem_limit_bytes=limit << 20),
    )(*args)
    return out[0] if one else out


def gather_call(cells, weights, st):
    return run(gather_kernel, [smem, vmem, vmem, vmem], (PIECES, V, SLOTS), [((ROWS + 8) * 8, NK)], 16, cells, cells, weights, st)


def scatter_call(cells, arrived, st):
    return run(
        scatter_kernel,
        [smem, vmem, vmem],
        [(CJ, V, NI + 16, NK), (2, V, NI, NK)],
        [((ROWS + 8) * 8, NK)],
        20,
        cells,
        arrived,
        st,
    )


def first_call(js, a, b, damp, field, low, high, inverse):
    def kernel(*refs):
        first_kernel(js, *refs)

    return run(
        kernel,
        [smem, smem, smem, vmem, vmem, vmem, vmem],
        (RANGES, V, len(js), CHUNK, NK),
        [(NI, V * NK)],
        20,
        a,
        b,
        damp,
        field,
        low,
        high,
        inverse,
    )


def second_call(inverse, lines):
    order = inverse.reshape(RANGES, CJ, RANGES, CJ).transpose(1, 0, 3, 2).reshape(NJ, NJ)
    rows = RANGES * V * CJ * CHUNK
    return run(
        second_kernel,
        [vmem, vmem],
        (rows, NK),
        [(NJ, CHUNK * NK), (NJ, CHUNK * NK)],
        20,
        order,
        lines.reshape(rows, NK),
    ).reshape(RANGES, V, CJ, CHUNK, NK)


def add_call(field, back):
    return run(add_kernel, [vmem, vmem], (V * ROWS, NK), [], 20, field, back)


def body(
    state,
    first_flux,
    second_flux,
    viscosity,
    first_inverse,
    second_inverse,
    donor_cell,
    donor_weight,
    receptor_cell,
):
    st = state.reshape(V * ROWS, NK)
    donated = gather_call(donor_cell[0], donor_weight[0], st)
    arrived = lax.all_to_all(donated, ("blk", "line"), split_axis=0, concat_axis=0, tiled=True)
    field, edges = scatter_call(receptor_cell[0], arrived, st)
    up = [(i, i + 1) for i in range(RANGES - 1)]
    down = [(i + 1, i) for i in range(RANGES - 1)]
    low = lax.ppermute(edges[1], "line", up)
    high = lax.ppermute(edges[0], "line", down)
    lines = first_call(
        range(CJ), first_flux, second_flux, viscosity, field, low, high, first_inverse[0]
    )
    lines = lax.all_to_all(lines, "line", split_axis=0, concat_axis=0, tiled=True)
    back = second_call(second_inverse[0], lines)
    back = lax.all_to_all(back, "line", split_axis=0, concat_axis=0, tiled=True)
    out = add_call(field, back)
    return out.reshape(1, V, NI, CJ, NK)


def solution(mesh):
    in_specs = (
        P("blk", None, None, "line", None),
        P("blk", None, None),
        P("blk", None, None),
        P("blk"),
        P("blk", None, None),
        P("blk", None, None),
        P(("blk", "line"), None, None),
        P(("blk", "line"), None, None),
        P(("blk", "line"), None, None),
    )
    out_specs = P("blk", None, None, "line", None)
    return jax.shard_map(body, mesh=mesh, in_specs=in_specs, out_specs=out_specs, check_vma=False)
```

time: 970 us -> 258 us (0.27)
  local copies, waits for them, and re-layouts: 816 us -> 5.9 us
  Pallas kernels: 0 us -> 124 us
  waiting for transfers between devices: 7.82 us -> 51.9 us
  other arithmetic: 39.1 us -> 0 us
  matrix products: 36.3 us -> 0 us
  blocking collectives: 40.2 us -> 61.5 us
  starting transfers between devices: 20.9 us -> 10.9 us
    gather x2 -> x0, local copies, waits for them, and re-layouts: 473 us -> none  [the longest x1 236 us: body(): second_value = jnp.take(local, cells_out + 1, axis=1)]
    scatter x2 -> x0, local copies, waits for them, and re-layouts: 178 us -> none  [body(): local.at[:, cells_in].set(arrived.reshape(variables, -1), mode='drop')]
    pallas_call x0 -> x5, Pallas kernels: none -> 124 us  [run(): pl.pallas_call(kernel, out_shape=[jax.ShapeDtypeStruct(s, f32) for s in s...]
    reshape x4 -> x1, local copies, waits for them, and re-layouts: 81.5 us -> 0.12 us  [second_call(): inverse.reshape(RANGES, CJ, RANGES, CJ).transpose(1, 0, 3, 2)]
    unnamed x17 -> x22, local copies, waits for them, and re-layouts: 50.7 us -> 4.94 us
    dot_general x4 -> x0, matrix products: 36.3 us -> none  [the longest x1 20.7 us: explicit_rhs(): jnp.einsum('uv,vijk->uijk', across_flux, plus_i - minus_i, precision=high...]
    all_to_all x2 -> x1, waiting for transfers between devices: 7.81 us -> 35.7 us  [body(): lax.all_to_all(lines, 'line', split_axis=0, concat_axis=0, tiled=True)]
    all_to_all x1 -> x2, blocking collectives: 40.2 us -> 61.5 us  [the longest x1 36.9 us: body(): back = lax.all_to_all(back, 'line', split_axis=0, concat_axis=0, tiled=True)]
  transfers between devices with their start and end apart: 4 -> 3, of which waited for: 2 -> 3; matrix products, arithmetic and copies ran while one was open for 9% -> 0% of each run, Pallas kernels for 0% -> 0%
where the time goes in v1:
time: 258 us; the launch traced here: 255 us
  Pallas kernels  124 us (48%)
  blocking collectives  61.5 us (24%)
  waiting for transfers between devices  51.9 us (20%)
  starting transfers between devices  10.9 us (4%)
  local copies, waits for them, and re-layouts  5.9 us (2%)
    pallas_call x5, Pallas kernels, run(): pl.pallas_call(kernel, out_shape=[jax.ShapeDtypeStruct(s, f32) for s in s...  124 us
    all_to_all x1, blocking collectives, body(): back = lax.all_to_all(back, 'line', split_axis=0, concat_axis=0, tiled=True)  36.9 us
    all_to_all x1, waiting for transfers between devices, body(): lax.all_to_all(lines, 'line', split_axis=0, concat_axis=0, tiled=True)  35.7 us
    all_to_all x1, blocking collectives, body(): lax.all_to_all(donated, ('blk', 'line'), split_axis=0, concat_axis=0, til...  24.6 us
    ppermute x1, waiting for transfers between devices, body(): low = lax.ppermute(edges[1], 'line', up)  12 us
    all_to_all x1, starting transfers between devices, body(): lax.all_to_all(lines, 'line', split_axis=0, concat_axis=0, tiled=True)  7.02 us
  transfers between devices with their start and end apart: 3, of which 3 were waited for; matrix products, arithmetic and copies ran while one was open for 0% of the time, Pallas kernels for 0%

profile of v1, /device:TPU:0, one launch (start us, length us, event | category | flops | bytes accessed | tf_op | source)
XLA Modules:
  0.0 255.4 jit_solution(12136713767791056834)
XLA Ops:
  0.0 0.0 copy-start
  0.0 1.7 copy-done
  1.7 0.0 copy-start.4
  1.7 0.8 copy-done.4
  2.6 0.0 copy-start.5
  2.6 0.8 copy-done.5
  3.4 0.0 copy-start.1
  3.4 0.0 copy-start.6
  3.4 57.3 %shard_map.91 = f32[128,5,128]{2,1,0:T(8,128)S(1)} custom-call(s32[128,128]{1,0:T(8,128)S(1)} %bitcast.17, s32[128,128]{1,0:T(8,128)S(1)} %bitcast.18, f32[128,128]{1,0:T(8,128)S(1)} %bitcast.19, f32[5120,128]{1,0:T(8,128)S(1)} %bitcast.13), custom_call_target="tpu_custom_call" | custom-call | tf_op jit(solution)/shard_map/pallas_call | solution.py:169
  60.7 24.6 %all_to_all.15.arrived_ref = f32[128,5,128]{2,1,0:T(8,128)S(1)} all-to-all(f32[128,5,128]{2,1,0:T(8,128)S(1)} %shard_map.91), channel_id=1, replica_groups=mesh['blk'=8,'line'=16] {'blk','line'}, dimensions={0} | all-to-all | bytes 655360 | tf_op jit(solution)/shard_map/all_to_all | solution.py:248
  85.3 0.0 copy-done.1
  85.3 0.0 copy-done.6
  85.3 0.0 copy-start.8
  85.3 0.0 copy-start.9
  85.3 0.0 copy-start.3
  85.3 42.8 %shard_map.92 = (f32[4,5,272,128]{3,2,1,0:T(8,128)S(1)}, f32[2,5,256,128]{3,2,1,0:T(8,128)S(1)}) custom-call(s32[128,128]{1,0:T(8,128)S(1)} %bitcast.20, f32[128,5,128]{2,1,0:T(8,128)S(1)} %all_to_all.15.arrived_ref, f32[5120,128]{1,0:T(8,128)S(1)} %bitcast.14), custom_call_target="tpu_custom_call" | custom-call | tf_op jit(solution)/shard_map/pallas_call | solution.py:169
  128.2 0.1 slice_bitcast_fusion
  128.3 2.6 %collective-permute-start = (f32[5,256,128]{2,1,0:T(8,128)S(1)}, f32[5,256,128]{2,1,0:T(8,128)S(1)}, u32[]{:S(2)}, u32[]{:S(2)}) collective-permute-start(f32[5,256,128]{2,1,0:T(8,128)S(1)} %get-tuple-element.10), channel_id=1, source_target_pairs={{0,1},{1,2},{2,3},{3,4},{4,5},{5,6},{6,7},{7,8},{8,9},{9,10},{10,1... | collective-permute-start | bytes 1966088 | tf_op jit(solution)/shard_map/ppermute | solution.py:252
  130.9 1.3 collective-permute-start.1
  132.2 0.0 copy-done.8
  132.2 0.0 copy-done.9
  132.8 12.0 %collective-permute-done.refs_4_ = f32[5,256,128]{2,1,0:T(8,128)S(1)} collective-permute-done((f32[5,256,128]{2,1,0:T(8,128)S(1)}, f32[5,256,128]{2,1,0:T(8,128)S(1)}, u32[]{:S(2)}, u32[]{:S(2)}) %collective-permute-start) | collective-permute-done | bytes 655392 | tf_op jit(solution)/shard_map/ppermute | solution.py:252
  144.9 4.2 %collective-permute-done.1.refs_5_ = f32[5,256,128]{2,1,0:T(8,128)S(1)} collective-permute-done((f32[5,256,128]{2,1,0:T(8,128)S(1)}, f32[5,256,128]{2,1,0:T(8,128)S(1)}, u32[]{:S(2)}, u32[]{:S(2)}) %collective-permute-start.1) | collective-permute-done | bytes 655392 | tf_op jit(solution)/shard_map/ppermute | solution.py:253
  149.0 0.0 copy-done.3
  149.0 16.9 %shard_map.93 = f32[16,5,4,16,128]{4,3,2,1,0:T(8,128)S(1)} custom-call(f32[1,5,5]{2,1,0:T(8,128)S(1)} %copy.14.refs_0_, f32[1,5,5]{2,1,0:T(8,128)S(1)} %copy.15.refs_1_, f32[1]{0:T(128)S(6)} %copy.16.refs_2_, f32[4,5,272,128]{3,2,1,0:T(8,128)S(1)} %get-tuple-element.7.refs_3_.field_ref, f32[5,256,128]{2,1,0:T(8,128)S(1)} %collective-permute-done.refs_4_, ...), custom_call_target="tpu_custom_call" | custom-call | tf_op jit(solution)/shard_map/pallas_call | solution.py:169
  166.0 0.0 copy-start.2
  166.0 1.5 copy-done.2
  167.5 0.0 copy-start.7
  167.5 7.0 %all-to-all-start.1 = ((f32[16,5,4,16,128]{4,3,2,1,0:T(8,128)}), f32[16,5,4,16,128]{4,3,2,1,0:T(8,128)}, u32[]{:S(2)}, u32[]{:S(2)}) async-start(f32[16,5,4,16,128]{4,3,2,1,0:T(8,128)} %copy-done.2), calls=%async_computation.1 | async-start | bytes 5242880 | tf_op jit(solution)/shard_map/all_to_all | solution.py:257
  174.5 0.0 copy-done.7
  174.5 0.3 reshape_squeeze.3
  174.8 0.5 copy.13
  175.3 0.1 reshape.16.inverse_ref
  175.4 35.7 %all-to-all-done.1 = f32[16,5,4,16,128]{4,3,2,1,0:T(8,128)} async-done(((f32[16,5,4,16,128]{4,3,2,1,0:T(8,128)}), f32[16,5,4,16,128]{4,3,2,1,0:T(8,128)}, u32[]{:S(2)}, u32[]{:S(2)}) %all-to-all-start.1) | async-done | bytes 2621472 | tf_op jit(solution)/shard_map/all_to_all | solution.py:257
  211.1 5.5 %shard_map.94 = f32[5120,128]{1,0:T(8,128)S(1)} custom-call(f32[64,64]{1,0:T(8,128)S(1)} %reshape.16.inverse_ref, f32[5120,128]{1,0:T(8,128)} %bitcast.8.in_ref), custom_call_target="tpu_custom_call" | custom-call | tf_op jit(solution)/shard_map/pallas_call | solution.py:169
  216.6 36.9 %all_to_all.16.back_ref = f32[16,5,4,16,128]{4,3,2,1,0:T(8,128)S(1)} all-to-all(f32[16,5,4,16,128]{4,3,2,1,0:T(8,128)S(1)} %bitcast.15), channel_id=1, replica_groups=mesh['blk'=8,'line'=16] {'line'}, dimensions={0} | all-to-all | bytes 5242880 | tf_op jit(solution)/shard_map/all_to_all | solution.py:259
  253.5 1.8 shard_map.95
  (2 shorter events, 0.0 us)
Async XLA Ops:
  0.0 1.7 copy-start
  1.7 0.8 copy-start.4
  2.6 0.8 copy-start.5
  3.4 81.9 %copy-start.1 = (f32[1,5,256,4,128]{4,3,2,1,0:T(4,128)S(1)}, f32[1,5,256,4,128]{4,3,2,1,0:T(4,128)}, u32[]{:S(2)}) copy-start(f32[1,5,256,4,128]{4,3,2,1,0:T(4,128)} %param.9) | copy-start | bytes 7864324
  3.4 81.9 %copy-start.6 = (s32[1,128,128]{2,1,0:T(8,128)S(1)}, s32[1,128,128]{2,1,0:T(8,128)}, u32[]{:S(2)}) copy-start(s32[1,128,128]{2,1,0:T(8,128)} %param.17) | copy-start | bytes 196612
  85.3 46.9 %copy-start.8 = (f32[1,5,5]{2,0,1:T(1,128)S(1)}, f32[1,5,5]{2,0,1:T(1,128)}, u32[]{:S(2)}) copy-start(f32[1,5,5]{2,0,1:T(1,128)} %param.10) | copy-start | bytes 304
  85.3 46.9 %copy-start.9 = (f32[1,5,5]{2,0,1:T(1,128)S(1)}, f32[1,5,5]{2,0,1:T(1,128)}, u32[]{:S(2)}) copy-start(f32[1,5,5]{2,0,1:T(1,128)} %param.11) | copy-start | bytes 304
  85.3 63.7 %copy-start.3 = (f32[1,256,256]{2,1,0:T(8,128)S(1)}, f32[1,256,256]{2,1,0:T(8,128)}, u32[]{:S(2)}) copy-start(f32[1,256,256]{2,1,0:T(8,128)} %param.13) | copy-start | bytes 786436
  128.3 16.6 %collective-permute-start = (f32[5,256,128]{2,1,0:T(8,128)S(1)}, f32[5,256,128]{2,1,0:T(8,128)S(1)}, u32[]{:S(2)}, u32[]{:S(2)}) collective-permute-start(f32[5,256,128]{2,1,0:T(8,128)S(1)} %get-tuple-element.10), channel_id=1, source_target_pairs={{0,1},{1,2},{2,3},{3,4},{4,5},{5,6},{6,7},{7,8},{8,9},{9,10},{10,1... | collective-permute-start | bytes 1966088 | tf_op jit(solution)/shard_map/ppermute | solution.py:252
  130.9 18.2 %collective-permute-start.1 = (f32[5,256,128]{2,1,0:T(8,128)S(1)}, f32[5,256,128]{2,1,0:T(8,128)S(1)}, u32[]{:S(2)}, u32[]{:S(2)}) collective-permute-start(f32[5,256,128]{2,1,0:T(8,128)S(1)} %get-tuple-element.9), channel_id=1, source_target_pairs={{1,0},{2,1},{3,2},{4,3},{5,4},{6,5},{7,6},{8,7},{9,8},{10,9},{11,1... | collective-permute-start | bytes 1966088 | tf_op jit(solution)/shard_map/ppermute | solution.py:253
  166.0 1.5 copy-start.2
  167.5 7.0 %copy-start.7 = (f32[1,64,64]{2,1,0:T(8,128)S(1)}, f32[1,64,64]{2,1,0:T(8,128)}, u32[]{:S(2)}) copy-start(f32[1,64,64]{2,1,0:T(8,128)} %param.14) | copy-start | bytes 49156
  167.5 43.6 %all-to-all-start.1 = ((f32[16,5,4,16,128]{4,3,2,1,0:T(8,128)}), f32[16,5,4,16,128]{4,3,2,1,0:T(8,128)}, u32[]{:S(2)}, u32[]{:S(2)}) async-start(f32[16,5,4,16,128]{4,3,2,1,0:T(8,128)} %copy-done.2), calls=%async_computation.1 | async-start | bytes 5242880 | tf_op jit(solution)/shard_map/all_to_all | solution.py:257

commit v2 on v1

v2 whole, which is shorter than its diff:
```python
import jax
import jax.numpy as jnp
from jax import lax
from jax.experimental import pallas as pl
from jax.experimental.pallas import tpu as pltpu
from jax.sharding import PartitionSpec as P

V, NI, CJ, NK, PIECES, SLOTS, RANGES = 5, 256, 4, 128, 128, 128, 16
ROWS = NI * CJ
CHUNK = NI // RANGES
NJ = CJ * RANGES
highest = lax.Precision.HIGHEST
f32 = jnp.float32


def to_rows(st_ref, tiles):
    def one(b, carry):
        for v in range(V):
            tiles[pl.ds(b * 64 + v, 8, stride=8), :] = st_ref[pl.ds(v * ROWS + b * 8, 8), :]
        return carry

    lax.fori_loop(0, ROWS // 8, one, 0)


def tile_of(tiles, cell):
    return tiles.at[pl.ds(pl.multiple_of((cell >> 7) * 8, 8), 8), :]


def gather_kernel(cell_ref, lane_ref, weight_ref, st_ref, out_ref, tiles, want, mix, picked):
    to_rows(st_ref, tiles)
    lane = lax.broadcasted_iota(jnp.int32, (8, 128), 1)
    sub = lax.broadcasted_iota(jnp.int32, (8, 128), 0)
    odd = lane & 1
    half = lane >> 1
    even = (lane * 2) & 127

    def before(b, carry):
        for t in range(4):
            r = pl.ds(pl.multiple_of(b * 32 + t * 8, 8), 8)
            cells = lane_ref[r, :] & 127
            weights = weight_ref[r, :]
            for h in range(2):
                want[h, r, :] = jnp.take_along_axis(cells, half + 64 * h, axis=1) + odd
                w = jnp.take_along_axis(weights, half + 64 * h, axis=1)
                mix[h, r, :] = jnp.where(odd == 0, w, 1.0 - w)
        return carry

    lax.fori_loop(0, PIECES // 32, before, 0)

    def piece(m, carry):
        for h in range(2):
            index = jnp.broadcast_to(want[h, pl.ds(m, 1), :], (8, 128))
            acc = jnp.zeros((8, 128), f32)
            for q in range(64):
                x = tile_of(tiles, cell_ref[m, 64 * h + q])[...]
                acc = jnp.where(half == q, jnp.take_along_axis(x, index, axis=1), acc)
            picked[m, h] = acc * jnp.broadcast_to(mix[h, pl.ds(m, 1), :], (8, 128))
        return carry

    lax.fori_loop(0, PIECES, piece, 0, unroll=4)

    def after(b, carry):
        for t in range(8):
            sums = []
            for h in range(2):
                x = picked[b * 8 + t, h]
                x = x + pltpu.roll(x, 127, axis=1)
                sums.append(jnp.take_along_axis(x, even, axis=1))
            x = jnp.where(lane < 64, sums[0], sums[1])
            out_ref[b * 8 + t] = jnp.where(sub < V, x, 0.0)
        return carry

    lax.fori_loop(0, PIECES // 8, after, 0)


def scatter_kernel(offset_ref, cell_ref, arrived_ref, st_ref, field_ref, low_ref, high_ref, tiles, parts, ping, pong):
    to_rows(st_ref, tiles)
    sub = lax.broadcasted_iota(jnp.int32, (8, 128), 0)

    def build(b, carry):
        r = pl.ds(pl.multiple_of(b * 16, 16), 16)
        x = []
        for t in range(2):
            lanes = (cell_ref[pl.ds(2 * b + t, 1), :] & 127).astype(f32)
            values = arrived_ref[pl.ds(pl.multiple_of(b * 16 + t * 8, 8), 8), :]
            x.append(jnp.where(sub == V, jnp.broadcast_to(lanes, (8, 128)), values))
        x = jnp.concatenate(x, axis=0)
        coarse = x.astype(jnp.bfloat16)
        parts[r, 0:128] = coarse
        parts[r, 128:256] = (x - coarse.astype(f32)).astype(jnp.bfloat16)
        return carry

    lax.fori_loop(0, PIECES // 2, build, 0, unroll=4)
    lane = lax.broadcasted_iota(jnp.int32, (8, 128), 1).astype(f32)
    square = (2 * SLOTS, 2 * NK)
    code = (lax.broadcasted_iota(jnp.int32, square, 0) & 127) - (lax.broadcasted_iota(jnp.int32, square, 1) >> 7)

    def spread(pair, buffer):
        ones = jnp.where(code == 2 * pair, 1.0, 0.0).astype(jnp.bfloat16)
        buffer[...] = jnp.dot(parts[...], ones, preferred_element_type=f32)

    def put(pair, buffer):
        for c in range(2):
            columns = slice(c * 128, c * 128 + 128)
            for n in range(PIECES):
                offset = pl.multiple_of(offset_ref[2 * pair + c, n], 8)
                value = buffer[n * 8 : n * 8 + 8, columns]
                lanes = jnp.broadcast_to(buffer[n * 8 + V : n * 8 + V + 1, columns], (8, 128))
                pltpu.store(tiles.at[pl.ds(offset, 8), :], value, mask=lane == lanes)

    spread(0, ping)

    def both(i, carry):
        spread(2 * i + 1, pong)
        put(2 * i, ping)
        spread(2 * i + 2, ping)
        put(2 * i + 1, pong)
        return carry

    lax.fori_loop(0, SLOTS // 4, both, 0)
    zero = jnp.zeros((8, 128), f32)
    for j in range(CJ):
        for v in range(V):
            field_ref[j, v, pl.ds(0, 8), :] = zero
            field_ref[j, v, pl.ds(NI + 8, 8), :] = zero

    def one(b, carry):
        for j in range(CJ):
            for v in range(V):
                x = tiles[pl.ds(b * 256 + j * 8 + v, 8, stride=32), :]
                field_ref[j, v, pl.ds(pl.multiple_of(8 + b * 8, 8), 8), :] = x
                if j == 0:
                    low_ref[v, pl.ds(pl.multiple_of(b * 8, 8), 8), :] = x
                if j == CJ - 1:
                    high_ref[v, pl.ds(pl.multiple_of(b * 8, 8), 8), :] = x
        return carry

    lax.fori_loop(0, NI // 8, one, 0)


def first_kernel(js, a_ref, b_ref, damp_ref, field_ref, inverse_ref, low_ref, high_ref, out_ref, coarse, fine):
    rows = 16
    lane = lax.broadcasted_iota(jnp.int32, (rows, 128), 1)
    damp = damp_ref[0]
    a = [[0.5 * a_ref[0, u, v] for v in range(V)] for u in range(V)]
    b = [[0.5 * b_ref[0, u, v] for v in range(V)] for u in range(V)]
    matrix = inverse_ref[...]
    matrix_coarse = matrix.astype(jnp.bfloat16)
    matrix_fine = (matrix - matrix_coarse.astype(f32)).astype(jnp.bfloat16)

    def dot(x, y):
        return jnp.dot(x, y, preferred_element_type=f32)

    for slot, j in enumerate(js):

        def one(t, carry):
            base = pl.multiple_of(t * rows, rows)
            di, dj, lap = [], [], []
            for v in range(V):
                c = field_ref[j, v, pl.ds(base + 8, rows), :]
                im = field_ref[j, v, pl.ds(base + 7, rows), :]
                ip = field_ref[j, v, pl.ds(base + 9, rows), :]
                if j == 0:
                    jm = low_ref[v, pl.ds(base, rows), :]
                else:
                    jm = field_ref[j - 1, v, pl.ds(base + 8, rows), :]
                if j == CJ - 1:
                    jp = high_ref[v, pl.ds(base, rows), :]
                else:
                    jp = field_ref[j + 1, v, pl.ds(base + 8, rows), :]
                kp = jnp.where(lane == NK - 1, 0.0, pltpu.roll(c, NK - 1, axis=1))
                km = jnp.where(lane == 0, 0.0, pltpu.roll(c, 1, axis=1))
                lap.append(ip + im + jp + jm + kp + km - 6.0 * c)
                di.append(ip - im)
                dj.append(jp - jm)
            for u in range(V):
                r = damp * lap[u]
                for v in range(V):
                    r = r - (a[u][v] * di[v] + b[u][v] * dj[v])
                big = r.astype(jnp.bfloat16)
                coarse[slot, pl.ds(base, rows), pl.ds(u * NK, NK)] = big
                fine[slot, pl.ds(base, rows), pl.ds(u * NK, NK)] = (r - big.astype(f32)).astype(jnp.bfloat16)
            return carry

        lax.fori_loop(0, NI // rows, one, 0)
        x, y = coarse[slot], fine[slot]
        solved = dot(matrix_coarse, x) + (dot(matrix_coarse, y) + dot(matrix_fine, x))
        for u in range(V):
            out_ref[:, u, slot] = solved[:, u * NK : (u + 1) * NK].reshape(RANGES, CHUNK, NK)


def second_kernel(inverse_ref, middle_ref, edge_ref, out_ref, wide, solved):
    step = V * CJ * CHUNK
    half = V * 2 * CHUNK
    places = [(edge_ref, 0), (middle_ref, 0), (middle_ref, 1), (edge_ref, 1)]
    for v in range(V):
        for j in range(CJ):
            ref, slot = places[j]
            for i in range(CHUNK):
                for s in range(0, RANGES, 8):
                    start = s * half + (v * 2 + slot) * CHUNK + i
                    wide[j * RANGES + s : j * RANGES + s + 8, i * NK : (i + 1) * NK] = ref[
                        pl.ds(start, 8, stride=half), :
                    ]
        solved[...] = jnp.dot(inverse_ref[...], wide[...], precision=highest, preferred_element_type=f32)
        for j in range(CJ):
            for i in range(CHUNK):
                for s in range(0, RANGES, 8):
                    start = s * step + (v * CJ + j) * CHUNK + i
                    out_ref[pl.ds(start, 8, stride=step), :] = solved[
                        j * RANGES + s : j * RANGES + s + 8, i * NK : (i + 1) * NK
                    ]


def add_kernel(field_ref, back_ref, out_ref):
    def one(t, carry):
        for v in range(V):
            for j in range(CJ):
                for h in range(CHUNK // 8):
                    i = t * CHUNK + h * 8
                    x = field_ref[j, v, pl.ds(pl.multiple_of(i + 8, 8), 8), :] + back_ref[t, v, j, pl.ds(h * 8, 8), :]
                    out_ref[pl.ds(v * ROWS + i * CJ + j, 8, stride=CJ), :] = x
        return carry

    lax.fori_loop(0, RANGES, one, 0)


smem = pl.BlockSpec(memory_space=pltpu.SMEM)
vmem = pl.BlockSpec(memory_space=pltpu.VMEM)


def run(kernel, specs, shapes, scratch, limit, moved, *args):
    one = not isinstance(shapes, list)
    shapes = [shapes] if one else shapes
    out = pl.pallas_call(
        kernel,
        out_shape=[jax.ShapeDtypeStruct(s, f32) for s in shapes],
        in_specs=specs,
        out_specs=[vmem] * len(shapes),
        scratch_shapes=[pltpu.VMEM(s, t) for s, t in scratch],
        compiler_params=pltpu.CompilerParams(vmem_limit_bytes=limit << 20),
        cost_estimate=pl.CostEstimate(flops=0, bytes_accessed=moved << 20, transcendentals=0),
    )(*args)
    return out[0] if one else out


TILES = (((ROWS + 8) * 8, NK), f32)


def gather_call(cells, weights, st):
    scratch = [TILES, ((2, PIECES, NK), jnp.int32), ((2, PIECES, NK), f32), ((PIECES, 2, 8, NK), f32)]
    return run(gather_kernel, [smem, vmem, vmem, vmem], (PIECES, 8, SLOTS), scratch, 16, 90, cells, cells, weights, st)


def scatter_call(cells, arrived, st):
    offsets = ((cells >> 7) * 8).T
    wide = (PIECES * 8, 2 * NK)
    return run(
        scatter_kernel,
        [smem, vmem, vmem, vmem],
        [(CJ, V, NI + 16, NK), (V, NI, NK), (V, NI, NK)],
        [TILES, (wide, jnp.bfloat16), (wide, f32), (wide, f32)],
        24,
        100,
        offsets,
        cells,
        arrived.reshape(PIECES * 8, NK),
        st,
    )


def first_call(js, a, b, damp, field, inverse, *layers):
    def middle_kernel(a_ref, b_ref, damp_ref, field_ref, inverse_ref, out_ref, coarse, fine):
        first_kernel(js, a_ref, b_ref, damp_ref, field_ref, inverse_ref, None, None, out_ref, coarse, fine)

    def edge_kernel(*refs):
        first_kernel(js, *refs)

    pair = ((len(js), NI, V * NK), jnp.bfloat16)
    return run(
        edge_kernel if layers else middle_kernel,
        [smem, smem, smem] + [vmem] * (2 + len(layers)),
        (RANGES, V, len(js), CHUNK, NK),
        [pair, pair],
        16,
        20,
        a,
        b,
        damp,
        field,
        inverse,
        *layers,
    )


def second_call(inverse, middle, edge):
    order = inverse.reshape(RANGES, CJ, RANGES, CJ).transpose(1, 0, 3, 2).reshape(NJ, NJ)
    rows = RANGES * V * CJ * CHUNK
    wide = ((NJ, CHUNK * NK), f32)
    return run(
        second_kernel,
        [vmem, vmem, vmem],
        (rows, NK),
        [wide, wide],
        16,
        20,
        order,
        middle.reshape(rows // 2, NK),
        edge.reshape(rows // 2, NK),
    ).reshape(RANGES, V, CJ, CHUNK, NK)


def add_call(field, back):
    return run(add_kernel, [vmem, vmem], (V * ROWS, NK), [], 16, 7, field, back)


def exchange(x, axes):
    return lax.all_to_all(x, axes, split_axis=0, concat_axis=0, tiled=True)


def body(
    state,
    first_flux,
    second_flux,
    viscosity,
    first_inverse,
    second_inverse,
    donor_cell,
    donor_weight,
    receptor_cell,
):
    st = state.reshape(V * ROWS, NK)
    donated = gather_call(donor_cell[0], donor_weight[0], st)
    arrived = exchange(donated, ("blk", "line"))
    field, first_layer, last_layer = scatter_call(receptor_cell[0], arrived, st)
    low = lax.ppermute(last_layer, "line", [(i, i + 1) for i in range(RANGES - 1)])
    high = lax.ppermute(first_layer, "line", [(i + 1, i) for i in range(RANGES - 1)])
    shared = (first_flux, second_flux, viscosity, field, first_inverse[0])
    middle = exchange(first_call((1, 2), *shared), "line")
    edge = exchange(first_call((0, 3), *shared, low, high), "line")
    back = exchange(second_call(second_inverse[0], middle, edge), "line")
    return add_call(field, back).reshape(1, V, NI, CJ, NK)


def solution(mesh):
    in_specs = (
        P("blk", None, None, "line", None),
        P("blk", None, None),
        P("blk", None, None),
        P("blk"),
        P("blk", None, None),
        P("blk", None, None),
        P(("blk", "line"), None, None),
        P(("blk", "line"), None, None),
        P(("blk", "line"), None, None),
    )
    out_specs = P("blk", None, None, "line", None)
    return jax.shard_map(body, mesh=mesh, in_specs=in_specs, out_specs=out_specs, check_vma=False)
```

time: 258 us -> 215 us (0.83)
  Pallas kernels: 124 us -> 77.9 us
  blocking collectives: 61.5 us -> 37.1 us
  starting transfers between devices: 10.9 us -> 28.2 us
  waiting for transfers between devices: 51.9 us -> 59 us
  local copies, waits for them, and re-layouts: 5.9 us -> 11.7 us
    pallas_call x5 -> x6, Pallas kernels: 124 us -> 77.9 us  [run(): pl.pallas_call(kernel, out_shape=[jax.ShapeDtypeStruct(s, f32) for s in s...]
    all_to_all x2 -> x1, blocking collectives: 61.5 us -> 37.1 us  [exchange(): return lax.all_to_all(x, axes, split_axis=0, concat_axis=0, tiled=True)]
    all_to_all x1 -> x3, starting transfers between devices: 7.02 us -> 23.2 us  [exchange(): return lax.all_to_all(x, axes, split_axis=0, concat_axis=0, tiled=True)]
    ppermute x2, waiting for transfers between devices: 16.2 us -> 25.8 us  [the longest x1 25.4 us: body(): lax.ppermute(last_layer, 'line', [(i, i + 1) for i in range(RANGES - 1)])]
    unnamed x22 -> x32, local copies, waits for them, and re-layouts: 4.94 us -> 10.7 us
    all_to_all x1 -> x3, waiting for transfers between devices: 35.7 us -> 33.2 us  [exchange(): return lax.all_to_all(x, axes, split_axis=0, concat_axis=0, tiled=True)]
  transfers between devices with their start and end apart: 3 -> 5, of which waited for: 3 -> 4; matrix products, arithmetic and copies ran while one was open for 0% -> 0% of each run, Pallas kernels for 0% -> 2%
where the time goes in v2:
time: 215 us
  Pallas kernels  77.9 us (36%)
  waiting for transfers between devices  59 us (27%)
  blocking collectives  37.1 us (17%)
  starting transfers between devices  28.2 us (13%)
  local copies, waits for them, and re-layouts  11.7 us (5%)
    pallas_call x6, Pallas kernels, run(): pl.pallas_call(kernel, out_shape=[jax.ShapeDtypeStruct(s, f32) for s in s...  77.9 us
    all_to_all x1, blocking collectives, exchange(): return lax.all_to_all(x, axes, split_axis=0, concat_axis=0, tiled=True)  37.1 us
    all_to_all x3, waiting for transfers between devices, exchange(): return lax.all_to_all(x, axes, split_axis=0, concat_axis=0, tiled=True)  33.2 us
    ppermute x1, waiting for transfers between devices, body(): lax.ppermute(last_layer, 'line', [(i, i + 1) for i in range(RANGES - 1)])  25.4 us
    all_to_all x3, starting transfers between devices, exchange(): return lax.all_to_all(x, axes, split_axis=0, concat_axis=0, tiled=True)  23.2 us
    unnamed x32, local copies, waits for them, and re-layouts  10.7 us
  transfers between devices with their start and end apart: 5, of which 4 were waited for; matrix products, arithmetic and copies ran while one was open for 0% of the time, Pallas kernels for 2%

profile of v2, /device:TPU:0, one launch (start us, length us, event | category | flops | bytes accessed | tf_op | source)
XLA Modules:
  0.0 214.8 jit_solution(1251070243015898462)
XLA Ops:
  0.0 0.0 copy-start.13
  0.0 0.0 copy-start.14
  0.0 0.0 copy-start
  0.0 1.8 copy-done
  1.8 0.0 copy-start.7
  1.8 0.8 copy-done.7
  2.6 0.0 copy-start.9
  2.6 0.8 copy-done.9
  3.5 0.0 copy-start.8
  3.5 29.5 %shard_map.91 = f32[128,8,128]{2,1,0:T(8,128)S(1)} custom-call(s32[128,128]{1,0:T(8,128)S(1)} %bitcast.20, s32[128,128]{1,0:T(8,128)S(1)} %bitcast.21, f32[128,128]{1,0:T(8,128)S(1)} %bitcast.23, f32[5120,128]{1,0:T(8,128)S(1)} %bitcast.14), custom_call_target="tpu_custom_call" | custom-call | bytes 94371840 | tf_op jit(solution)/shard_map/pallas_call | solution.py:235
  33.0 0.0 copy-start.4
  33.0 0.8 copy-done.4
  33.8 11.1 %all-to-all-start = ((f32[128,8,128]{2,1,0:T(8,128)}), f32[128,8,128]{2,1,0:T(8,128)S(1)}, u32[]{:S(2)}, u32[]{:S(2)}) async-start(f32[128,8,128]{2,1,0:T(8,128)} %copy-done.4), calls=%async_computation | async-start | bytes 1048576 | tf_op jit(solution)/shard_map/all_to_all | solution.py:318
  45.5 0.0 copy-done.13
  45.6 0.0 copy-done.14
  45.6 0.0 copy-done.8
  45.6 0.1 copy.16.offset_ref
  45.7 12.8 %all-to-all-done = f32[128,8,128]{2,1,0:T(8,128)S(1)} async-done(((f32[128,8,128]{2,1,0:T(8,128)}), f32[128,8,128]{2,1,0:T(8,128)S(1)}, u32[]{:S(2)}, u32[]{:S(2)}) %all-to-all-start) | async-done | bytes 524320 | tf_op jit(solution)/shard_map/all_to_all | solution.py:318
  58.5 0.0 copy-start.1
  58.5 1.7 copy-done.1
  60.2 30.6 %shard_map.92 = (f32[4,5,272,128]{3,2,1,0:T(8,128)S(1)}, f32[5,256,128]{2,1,0:T(8,128)S(1)}, f32[5,256,128]{2,1,0:T(8,128)S(1)}) custom-call(s32[128,128]{1,0:T(8,128)S(1)} %copy.16.offset_ref, s32[128,128]{1,0:T(8,128)S(1)} %bitcast.22, f32[1024,128]{1,0:T(8,128)S(1)} %bitcast.17, f32[5120,128]{1,0:T(8,128)S(1)} %bitcast.15), custom_call_target="tpu_custom_call" | custom-call | bytes 104857600 | tf_op jit(solution)/shard_map/pallas_call | solution.py:235
  90.9 0.0 copy-start.10
  90.9 0.8 copy-done.10
  91.7 0.0 copy-start.11
  91.7 0.8 copy-done.11
  92.6 0.0 copy-start.5
  92.6 0.9 copy-done.5
  93.5 0.0 copy-start.6
  93.5 5.2 %shard_map.93 = f32[16,5,2,16,128]{4,3,2,1,0:T(8,128)S(1)} custom-call(f32[1,5,5]{2,1,0:T(8,128)S(1)} %copy.18.a_ref.refs_0_, f32[1,5,5]{2,1,0:T(8,128)S(1)} %copy.19.b_ref.refs_1_, f32[1]{0:T(128)S(6)} %copy.22.damp_ref.refs_2_, f32[4,5,272,128]{3,2,1,0:T(8,128)S(1)} %get-tuple-element.8.field_ref.refs_3_, f32[256,256]{1,0:T(8,128)S(1)} %bitcast.18), custom_call_target="tpu_custom_call" | custom-call | bytes 20971520 | tf_op jit(solution)/shard_map/pallas_call | solution.py:235
  98.7 0.0 copy-start.2
  98.7 1.0 copy-done.2
  99.8 4.4 %all-to-all-start.1 = ((f32[16,5,2,16,128]{4,3,2,1,0:T(8,128)}), f32[16,5,2,16,128]{4,3,2,1,0:T(8,128)}, u32[]{:S(2)}, u32[]{:S(2)}) async-start(f32[16,5,2,16,128]{4,3,2,1,0:T(8,128)} %copy-done.2), calls=%async_computation.1 | async-start | bytes 2621440 | tf_op jit(solution)/shard_map/all_to_all | solution.py:318
  104.2 3.7 %collective-permute-start = (f32[5,256,128]{2,1,0:T(8,128)}, f32[5,256,128]{2,1,0:T(8,128)S(1)}, u32[]{:S(2)}, u32[]{:S(2)}) collective-permute-start(f32[5,256,128]{2,1,0:T(8,128)} %copy-done.11), channel_id=1, source_target_pairs={{0,1},{1,2},{2,3},{3,4},{4,5},{5,6},{6,7},{7,8},{8,9},{9,10},{10,1... | collective-permute-start | bytes 1966088 | tf_op jit(solution)/shard_map/ppermute | solution.py:336
  107.9 1.3 collective-permute-start.1
  109.2 25.4 %collective-permute-done.refs_5_ = f32[5,256,128]{2,1,0:T(8,128)S(1)} collective-permute-done((f32[5,256,128]{2,1,0:T(8,128)}, f32[5,256,128]{2,1,0:T(8,128)S(1)}, u32[]{:S(2)}, u32[]{:S(2)}) %collective-permute-start) | collective-permute-done | bytes 655392 | tf_op jit(solution)/shard_map/ppermute | solution.py:336
  134.6 0.3 collective-permute-done.1.refs_6_
  135.0 0.0 copy-done.6
  135.0 5.2 %shard_map.94 = f32[16,5,2,16,128]{4,3,2,1,0:T(8,128)S(1)} custom-call(f32[1,5,5]{2,1,0:T(8,128)S(1)} %copy.18.a_ref.refs_0_, f32[1,5,5]{2,1,0:T(8,128)S(1)} %copy.19.b_ref.refs_1_, f32[1]{0:T(128)S(6)} %copy.22.damp_ref.refs_2_, f32[4,5,272,128]{3,2,1,0:T(8,128)S(1)} %get-tuple-element.8.field_ref.refs_3_, f32[256,256]{1,0:T(8,128)S(1)} %bitcast.19, ...), custom_call_target="tpu_custom_call" | custom-call | bytes 20971520 | tf_op jit(solution)/shard_map/pallas_call | solution.py:235
  140.1 0.0 copy-start.3
  140.2 1.1 copy-done.3
  141.2 0.0 copy-start.12
  141.2 0.0 all-to-all-done.1
  141.2 7.7 %all-to-all-start.2 = ((f32[16,5,2,16,128]{4,3,2,1,0:T(8,128)}), f32[16,5,2,16,128]{4,3,2,1,0:T(8,128)}, u32[]{:S(2)}, u32[]{:S(2)}) async-start(f32[16,5,2,16,128]{4,3,2,1,0:T(8,128)} %copy-done.3), calls=%async_computation.2 | async-start | bytes 2621440 | tf_op jit(solution)/shard_map/all_to_all | solution.py:318
  148.9 0.0 copy-done.12
  148.9 0.3 reshape_squeeze.3
  149.2 0.5 copy.17
  149.7 0.1 reshape.23.inverse_ref
  149.8 20.4 %all-to-all-done.2 = f32[16,5,2,16,128]{4,3,2,1,0:T(8,128)} async-done(((f32[16,5,2,16,128]{4,3,2,1,0:T(8,128)}), f32[16,5,2,16,128]{4,3,2,1,0:T(8,128)}, u32[]{:S(2)}, u32[]{:S(2)}) %all-to-all-start.2) | async-done | bytes 1310752 | tf_op jit(solution)/shard_map/all_to_all | solution.py:318
  170.3 5.5 %shard_map.95 = f32[5120,128]{1,0:T(8,128)S(1)} custom-call(f32[64,64]{1,0:T(8,128)S(1)} %reshape.23.inverse_ref, f32[2560,128]{1,0:T(8,128)} %bitcast.8.middle_ref, f32[2560,128]{1,0:T(8,128)} %bitcast.9.edge_ref), custom_call_target="tpu_custom_call" | custom-call | bytes 20971520 | tf_op jit(solution)/shard_map/pallas_call | solution.py:235
  175.8 37.1 %all_to_all.20.back_ref = f32[16,5,4,16,128]{4,3,2,1,0:T(8,128)S(1)} all-to-all(f32[16,5,4,16,128]{4,3,2,1,0:T(8,128)S(1)} %bitcast.16), channel_id=1, replica_groups=mesh['blk'=8,'line'=16] {'line'}, dimensions={0} | all-to-all | bytes 5242880 | tf_op jit(solution)/shard_map/all_to_all | solution.py:318
  212.9 1.8 shard_map.96
  (3 shorter events, 0.0 us)
Async XLA Ops:
  0.0 45.5 %copy-start.13 = (f32[1,5,5]{2,0,1:T(1,128)S(1)}, f32[1,5,5]{2,0,1:T(1,128)}, u32[]{:S(2)}) copy-start(f32[1,5,5]{2,0,1:T(1,128)} %param.10) | copy-start | bytes 304
  0.0 45.6 %copy-start.14 = (f32[1,5,5]{2,0,1:T(1,128)S(1)}, f32[1,5,5]{2,0,1:T(1,128)}, u32[]{:S(2)}) copy-start(f32[1,5,5]{2,0,1:T(1,128)} %param.11) | copy-start | bytes 304
  0.0 1.8 copy-start
  1.8 0.8 copy-start.7
  2.6 0.8 copy-start.9
  3.5 42.1 %copy-start.8 = (s32[1,128,128]{2,1,0:T(8,128)S(1)}, s32[1,128,128]{2,1,0:T(8,128)}, u32[]{:S(2)}) copy-start(s32[1,128,128]{2,1,0:T(8,128)} %param.17) | copy-start | bytes 196612
  33.0 0.8 copy-start.4
  33.8 24.8 %all-to-all-start = ((f32[128,8,128]{2,1,0:T(8,128)}), f32[128,8,128]{2,1,0:T(8,128)S(1)}, u32[]{:S(2)}, u32[]{:S(2)}) async-start(f32[128,8,128]{2,1,0:T(8,128)} %copy-done.4), calls=%async_computation | async-start | bytes 1048576 | tf_op jit(solution)/shard_map/all_to_all | solution.py:318
  58.5 1.7 copy-start.1
  90.9 0.9 copy-start.10
  91.7 0.8 copy-start.11
  92.6 0.9 copy-start.5
  93.5 41.4 %copy-start.6 = (f32[1,256,256]{2,1,0:T(8,128)S(1)}, f32[1,256,256]{2,1,0:T(8,128)}, u32[]{:S(2)}) copy-start(f32[1,256,256]{2,1,0:T(8,128)} %param.13) | copy-start | bytes 786436
  98.7 1.1 copy-start.2
  99.8 41.4 %all-to-all-start.1 = ((f32[16,5,2,16,128]{4,3,2,1,0:T(8,128)}), f32[16,5,2,16,128]{4,3,2,1,0:T(8,128)}, u32[]{:S(2)}, u32[]{:S(2)}) async-start(f32[16,5,2,16,128]{4,3,2,1,0:T(8,128)} %copy-done.2), calls=%async_computation.1 | async-start | bytes 2621440 | tf_op jit(solution)/shard_map/all_to_all | solution.py:318
  104.2 30.4 %collective-permute-start = (f32[5,256,128]{2,1,0:T(8,128)}, f32[5,256,128]{2,1,0:T(8,128)S(1)}, u32[]{:S(2)}, u32[]{:S(2)}) collective-permute-start(f32[5,256,128]{2,1,0:T(8,128)} %copy-done.11), channel_id=1, source_target_pairs={{0,1},{1,2},{2,3},{3,4},{4,5},{5,6},{6,7},{7,8},{8,9},{9,10},{10,1... | collective-permute-start | bytes 1966088 | tf_op jit(solution)/shard_map/ppermute | solution.py:336
  107.9 27.1 %collective-permute-start.1 = (f32[5,256,128]{2,1,0:T(8,128)}, f32[5,256,128]{2,1,0:T(8,128)S(1)}, u32[]{:S(2)}, u32[]{:S(2)}) collective-permute-start(f32[5,256,128]{2,1,0:T(8,128)} %copy-done.10), channel_id=1, source_target_pairs={{1,0},{2,1},{3,2},{4,3},{5,4},{6,5},{7,6},{8,7},{9,8},{10,9},{11,1... | collective-permute-start | bytes 1966088 | tf_op jit(solution)/shard_map/ppermute | solution.py:337
  140.1 1.1 copy-start.3
  141.2 7.7 %copy-start.12 = (f32[1,64,64]{2,1,0:T(8,128)S(1)}, f32[1,64,64]{2,1,0:T(8,128)}, u32[]{:S(2)}) copy-start(f32[1,64,64]{2,1,0:T(8,128)} %param.14) | copy-start | bytes 49156
  141.2 29.1 %all-to-all-start.2 = ((f32[16,5,2,16,128]{4,3,2,1,0:T(8,128)}), f32[16,5,2,16,128]{4,3,2,1,0:T(8,128)}, u32[]{:S(2)}, u32[]{:S(2)}) async-start(f32[16,5,2,16,128]{4,3,2,1,0:T(8,128)} %copy-done.3), calls=%async_computation.2 | async-start | bytes 2621440 | tf_op jit(solution)/shard_map/all_to_all | solution.py:318

commit v3 on v2

v3 whole, which is shorter than its diff:
```python
import jax
import jax.numpy as jnp
from jax import lax
from jax.experimental import pallas as pl
from jax.experimental.pallas import tpu as pltpu
from jax.sharding import PartitionSpec as P

V, NI, CJ, NK, PIECES, SLOTS, RANGES = 5, 256, 4, 128, 128, 128, 16
ROWS = NI * CJ
DEPTH = (ROWS + 8) * 8
CHUNK = NI // RANGES
NJ = CJ * RANGES
highest = lax.Precision.HIGHEST
f32 = jnp.float32


def gather_kernel(offset_ref, lane_ref, weight_ref, st_ref, out_ref, kept_ref, tiles, want, mix, picked, sem):
    lane = lax.broadcasted_iota(jnp.int32, (8, 128), 1)
    sub = lax.broadcasted_iota(jnp.int32, (8, 128), 0)
    odd = lane & 1
    half = lane >> 1
    even = (lane * 2) & 127
    def lay(b, carry):
        for t in range(2):
            c = b * 2 + t
            for v in range(V):
                tiles[pl.ds(c * 64 + v, 8, stride=8), :] = st_ref[
                    pl.ds(pl.multiple_of(v * ROWS + c * 8, 8), 8), :
                ]
        return carry

    lax.fori_loop(0, ROWS // 16, lay, 0)
    keep = pltpu.make_async_copy(tiles, kept_ref, sem)
    keep.start()

    def before(b, carry):
        for t in range(4):
            r = pl.ds(pl.multiple_of(b * 32 + t * 8, 8), 8)
            cells = lane_ref[r, :] & 127
            weights = weight_ref[r, :]
            for h in range(2):
                want[h, r, :] = jnp.take_along_axis(cells, half + 64 * h, axis=1) + odd
                w = jnp.take_along_axis(weights, half + 64 * h, axis=1)
                mix[h, r, :] = jnp.where(odd == 0, w, 1.0 - w)
        return carry

    lax.fori_loop(0, PIECES // 32, before, 0)

    def piece(m, carry):
        for h in range(2):
            index = jnp.broadcast_to(want[h, pl.ds(m, 1), :], (8, 128))
            acc = jnp.zeros((8, 128), f32)
            for q in range(64):
                x = tiles[pl.ds(pl.multiple_of(offset_ref[m, 64 * h + q], 8), 8), :]
                acc = jnp.where(half == q, jnp.take_along_axis(x, index, axis=1), acc)
            picked[m, h] = acc * jnp.broadcast_to(mix[h, pl.ds(m, 1), :], (8, 128))
        return carry

    lax.fori_loop(0, PIECES, piece, 0, unroll=8)

    def after(b, carry):
        for t in range(16):
            sums = []
            for h in range(2):
                x = picked[b * 16 + t, h]
                x = x + pltpu.roll(x, 127, axis=1)
                sums.append(jnp.take_along_axis(x, even, axis=1))
            x = jnp.where(lane < 64, sums[0], sums[1])
            out_ref[b * 16 + t] = jnp.where(sub < V, x, 0.0)
        return carry

    lax.fori_loop(0, PIECES // 16, after, 0)
    keep.wait()


def scatter_kernel(offset_ref, cell_ref, arrived_ref, kept_ref, field_ref, low_ref, high_ref, tiles, parts, ping, pong, sem):
    keep = pltpu.make_async_copy(kept_ref, tiles, sem)
    keep.start()
    sub = lax.broadcasted_iota(jnp.int32, (8, 128), 0)

    def build(b, carry):
        r = pl.ds(pl.multiple_of(b * 16, 16), 16)
        x = []
        for t in range(2):
            lanes = (cell_ref[pl.ds(2 * b + t, 1), :] & 127).astype(f32)
            values = arrived_ref[pl.ds(pl.multiple_of(b * 16 + t * 8, 8), 8), :]
            x.append(jnp.where(sub == V, jnp.broadcast_to(lanes, (8, 128)), values))
        x = jnp.concatenate(x, axis=0)
        coarse = x.astype(jnp.bfloat16)
        parts[r, 0:128] = coarse
        parts[r, 128:256] = (x - coarse.astype(f32)).astype(jnp.bfloat16)
        return carry

    lax.fori_loop(0, PIECES // 2, build, 0, unroll=4)
    lane = lax.broadcasted_iota(jnp.int32, (8, 128), 1).astype(f32)
    square = (2 * SLOTS, 2 * NK)
    code = (lax.broadcasted_iota(jnp.int32, square, 0) & 127) - (lax.broadcasted_iota(jnp.int32, square, 1) >> 7)
    group = PIECES // 4

    def ones(pair):
        return jnp.where(code == 2 * pair, 1.0, 0.0).astype(jnp.bfloat16)

    def spread(mask, buffer, g):
        rows = slice(g * group * 8, (g + 1) * group * 8)
        buffer[rows, :] = jnp.dot(parts[rows, :], mask, preferred_element_type=f32)

    def put(pair, buffer, g):
        for n in range(g * group, (g + 1) * group):
            for c in range(2):
                columns = slice(c * 128, c * 128 + 128)
                offset = pl.multiple_of(offset_ref[2 * pair + c, n], 8)
                value = buffer[n * 8 : n * 8 + 8, columns]
                lanes = jnp.broadcast_to(buffer[n * 8 + V : n * 8 + V + 1, columns], (8, 128))
                pltpu.store(tiles.at[pl.ds(offset, 8), :], value, mask=lane == lanes)

    def step(pair, now, later):
        mask = ones(pair + 1)
        for g in range(4):
            spread(mask, later, g)
            put(pair, now, g)

    first = ones(0)
    for g in range(4):
        spread(first, ping, g)
    keep.wait()

    def both(i, carry):
        step(2 * i, ping, pong)
        step(2 * i + 1, pong, ping)
        return carry

    lax.fori_loop(0, SLOTS // 4, both, 0)
    zero = jnp.zeros((8, 128), f32)
    for j in range(CJ):
        for v in range(V):
            field_ref[j, v, pl.ds(0, 8), :] = zero
            field_ref[j, v, pl.ds(NI + 8, 8), :] = zero

    def one(b, carry):
        for j in range(CJ):
            for v in range(V):
                x = tiles[pl.ds(b * 256 + j * 8 + v, 8, stride=32), :]
                field_ref[j, v, pl.ds(pl.multiple_of(8 + b * 8, 8), 8), :] = x
                if j == 0:
                    low_ref[v, pl.ds(pl.multiple_of(b * 8, 8), 8), :] = x
                if j == CJ - 1:
                    high_ref[v, pl.ds(pl.multiple_of(b * 8, 8), 8), :] = x
        return carry

    lax.fori_loop(0, NI // 8, one, 0)


def first_kernel(js, a_ref, b_ref, damp_ref, field_ref, inverse_ref, low_ref, high_ref, put, coarse, fine):
    rows = 16
    lane = lax.broadcasted_iota(jnp.int32, (rows, 128), 1)
    damp = damp_ref[0]
    a = [[0.5 * a_ref[0, u, v] for v in range(V)] for u in range(V)]
    b = [[0.5 * b_ref[0, u, v] for v in range(V)] for u in range(V)]
    matrix = inverse_ref[...]
    matrix_coarse = matrix.astype(jnp.bfloat16)
    matrix_fine = (matrix - matrix_coarse.astype(f32)).astype(jnp.bfloat16)

    def dot(x, y):
        return jnp.dot(x, y, preferred_element_type=f32)

    for slot, j in enumerate(js):

        def one(t, carry):
            base = pl.multiple_of(t * rows, rows)

            def cells(v, di, j):
                return field_ref[j, v, pl.ds(base + 8 + di, rows), :]

            di, dj, lap = [], [], []
            for v in range(V):
                c = cells(v, 0, j)
                im = cells(v, -1, j)
                ip = cells(v, 1, j)
                jm = low_ref[v, pl.ds(base, rows), :] if j == 0 else cells(v, 0, j - 1)
                jp = high_ref[v, pl.ds(base, rows), :] if j == CJ - 1 else cells(v, 0, j + 1)
                kp = jnp.where(lane == NK - 1, 0.0, pltpu.roll(c, NK - 1, axis=1))
                km = jnp.where(lane == 0, 0.0, pltpu.roll(c, 1, axis=1))
                lap.append(ip + im + jp + jm + kp + km - 6.0 * c)
                di.append(ip - im)
                dj.append(jp - jm)
            for u in range(V):
                r = damp * lap[u]
                for v in range(V):
                    r = r - (a[u][v] * di[v] + b[u][v] * dj[v])
                big = r.astype(jnp.bfloat16)
                coarse[slot, pl.ds(base, rows), pl.ds(u * NK, NK)] = big
                fine[slot, pl.ds(base, rows), pl.ds(u * NK, NK)] = (r - big.astype(f32)).astype(jnp.bfloat16)
            return carry

        lax.fori_loop(0, NI // rows, one, 0)
        x, y = coarse[slot], fine[slot]
        solved = dot(matrix_coarse, x) + (dot(matrix_coarse, y) + dot(matrix_fine, x))
        for u in range(V):
            put(u, slot, j, solved[:, u * NK : (u + 1) * NK].reshape(RANGES, CHUNK, NK))


def middle_kernel(a_ref, b_ref, damp_ref, field_ref, inverse_ref, out_ref, coarse, fine):
    def put(u, slot, j, value):
        out_ref[:, u, slot] = value

    first_kernel((1, 2), a_ref, b_ref, damp_ref, field_ref, inverse_ref, None, None, put, coarse, fine)


def edge_kernel(a_ref, b_ref, damp_ref, field_ref, inverse_ref, low_ref, high_ref, middle_ref, out_ref, coarse, fine):
    def put(u, slot, j, value):
        out_ref[:, u, j] = value

    for u in range(V):
        out_ref[:, u, 1:3] = middle_ref[:, u]
    first_kernel((0, 3), a_ref, b_ref, damp_ref, field_ref, inverse_ref, low_ref, high_ref, put, coarse, fine)


def second_kernel(inverse_ref, in_ref, out_ref, wide, solved):
    step = V * CJ * CHUNK
    for v in range(V):
        for j in range(CJ):
            for i in range(CHUNK):
                for s in range(0, RANGES, 8):
                    start = s * step + (v * CJ + j) * CHUNK + i
                    wide[j * RANGES + s : j * RANGES + s + 8, i * NK : (i + 1) * NK] = in_ref[
                        pl.ds(start, 8, stride=step), :
                    ]
        solved[...] = jnp.dot(inverse_ref[...], wide[...], precision=highest, preferred_element_type=f32)
        for j in range(CJ):
            for i in range(CHUNK):
                for s in range(0, RANGES, 8):
                    start = s * step + (v * CJ + j) * CHUNK + i
                    out_ref[pl.ds(start, 8, stride=step), :] = solved[
                        j * RANGES + s : j * RANGES + s + 8, i * NK : (i + 1) * NK
                    ]


def add_kernel(field_ref, back_ref, out_ref):
    def one(t, carry):
        for v in range(V):
            for j in range(CJ):
                for h in range(CHUNK // 8):
                    i = t * CHUNK + h * 8
                    x = field_ref[j, v, pl.ds(pl.multiple_of(i + 8, 8), 8), :] + back_ref[t, v, j, pl.ds(h * 8, 8), :]
                    out_ref[pl.ds(v * ROWS + i * CJ + j, 8, stride=CJ), :] = x
        return carry

    lax.fori_loop(0, RANGES, one, 0)


smem = pl.BlockSpec(memory_space=pltpu.SMEM)
vmem = pl.BlockSpec(memory_space=pltpu.VMEM)
hbm = pl.BlockSpec(memory_space=pltpu.HBM)


def run(kernel, specs, shapes, scratch, limit, *args, outs=None, sems=0):
    one = not isinstance(shapes, list)
    shapes = [shapes] if one else shapes
    out = pl.pallas_call(
        kernel,
        out_shape=[jax.ShapeDtypeStruct(s, f32) for s in shapes],
        in_specs=specs,
        out_specs=outs or [vmem] * len(shapes),
        scratch_shapes=[pltpu.VMEM(s, t) for s, t in scratch] + [pltpu.SemaphoreType.DMA] * sems,
        compiler_params=pltpu.CompilerParams(vmem_limit_bytes=limit << 20),
    )(*args)
    return out[0] if one else out


def offsets_of(cells):
    return (cells >> 7) * 8


def gather_call(cells, weights, st):
    scratch = [((DEPTH, NK), f32), ((2, PIECES, NK), jnp.int32), ((2, PIECES, NK), f32), ((PIECES, 2, 8, NK), f32)]
    shapes = [(PIECES, 8, SLOTS), (DEPTH, NK)]
    specs = [smem, vmem, vmem, vmem]
    args = (offsets_of(cells), cells, weights, st)
    return run(gather_kernel, specs, shapes, scratch, 48, *args, outs=[vmem, hbm], sems=1)


def scatter_call(cells, arrived, kept):
    wide = (PIECES * 8, 2 * NK)
    return run(
        scatter_kernel,
        [smem, vmem, vmem, hbm],
        [(CJ, V, NI + 16, NK), (V, NI, NK), (V, NI, NK)],
        [((DEPTH, NK), f32), (wide, jnp.bfloat16), (wide, f32), (wide, f32)],
        48,
        offsets_of(cells).T,
        cells,
        arrived.reshape(PIECES * 8, NK),
        kept,
        sems=1,
    )


def middle_call(*shared):
    pair = ((2, NI, V * NK), jnp.bfloat16)
    return run(middle_kernel, [smem] * 3 + [vmem] * 2, (RANGES, V, 2, CHUNK, NK), [pair, pair], 20, *shared)


def edge_call(*shared):
    pair = ((2, NI, V * NK), jnp.bfloat16)
    return run(edge_kernel, [smem] * 3 + [vmem] * 5, (RANGES, V, CJ, CHUNK, NK), [pair, pair], 20, *shared)


def ordered(inverse):
    return inverse.reshape(RANGES, CJ, RANGES, CJ).transpose(1, 0, 3, 2).reshape(NJ, NJ)


def second_call(order, lines):
    rows = RANGES * V * CJ * CHUNK
    wide = ((NJ, CHUNK * NK), f32)
    out = run(second_kernel, [vmem, vmem], (rows, NK), [wide, wide], 20, order, lines.reshape(rows, NK))
    return out.reshape(RANGES, V, CJ, CHUNK, NK)


def add_call(field, back):
    return run(add_kernel, [vmem, vmem], (V * ROWS, NK), [], 20, field, back)


def exchange(x, axes):
    return lax.all_to_all(x, axes, split_axis=0, concat_axis=0, tiled=True)


def body(
    state,
    first_flux,
    second_flux,
    viscosity,
    first_inverse,
    second_inverse,
    donor_cell,
    donor_weight,
    receptor_cell,
):
    st = state.reshape(V * ROWS, NK)
    donated, kept = gather_call(donor_cell[0], donor_weight[0], st)
    arrived = exchange(donated, ("blk", "line"))
    field, first_layer, last_layer = scatter_call(receptor_cell[0], arrived, kept)
    low = lax.ppermute(last_layer, "line", [(i, i + 1) for i in range(RANGES - 1)])
    high = lax.ppermute(first_layer, "line", [(i + 1, i) for i in range(RANGES - 1)])
    shared = (first_flux, second_flux, viscosity, field, first_inverse[0])
    middle = middle_call(*shared)
    order = ordered(second_inverse[0])
    lines, order = lax.optimization_barrier((edge_call(*shared, low, high, middle), order))
    lines = exchange(lines, "line")
    back = exchange(second_call(order, lines), "line")
    return add_call(field, back).reshape(1, V, NI, CJ, NK)


def solution(mesh):
    in_specs = (
        P("blk", None, None, "line", None),
        P("blk", None, None),
        P("blk", None, None),
        P("blk"),
        P("blk", None, None),
        P("blk", None, None),
        P(("blk", "line"), None, None),
        P(("blk", "line"), None, None),
        P(("blk", "line"), None, None),
    )
    out_specs = P("blk", None, None, "line", None)
    return jax.shard_map(body, mesh=mesh, in_specs=in_specs, out_specs=out_specs, check_vma=False)
```

time: 215 us -> 189 us (0.88)
  waiting for transfers between devices: 59 us -> 19.5 us
  blocking collectives: 37.1 us -> 75.2 us
  starting transfers between devices: 28.2 us -> 15 us
  Pallas kernels: 77.9 us -> 67.8 us
  local copies, waits for them, and re-layouts: 11.7 us -> 8.72 us
    all_to_all x1 -> x2, blocking collectives: 37.1 us -> 75.2 us  [exchange(): return lax.all_to_all(x, axes, split_axis=0, concat_axis=0, tiled=True)]
    ppermute x1, waiting for transfers between devices: 25.4 us -> 1.91 us  [body(): lax.ppermute(last_layer, 'line', [(i, i + 1) for i in range(RANGES - 1)])]
    all_to_all x3 -> x1, waiting for transfers between devices: 33.2 us -> 13.4 us  [exchange(): return lax.all_to_all(x, axes, split_axis=0, concat_axis=0, tiled=True)]
    all_to_all x3 -> x1, starting transfers between devices: 23.2 us -> 11.1 us  [exchange(): return lax.all_to_all(x, axes, split_axis=0, concat_axis=0, tiled=True)]
    pallas_call x6, Pallas kernels: 77.9 us -> 67.8 us  [run(): pl.pallas_call(kernel, out_shape=[jax.ShapeDtypeStruct(s, f32) for s in s...]
    unnamed x32 -> x18, local copies, waits for them, and re-layouts: 10.7 us -> 4.39 us
    ppermute x1, waiting for transfers between devices: 0.34 us -> 4.16 us  [body(): lax.ppermute(first_layer, 'line', [(i + 1, i) for i in range(RANGES - 1)])]
  transfers between devices with their start and end apart: 5 -> 3, of which waited for: 4 -> 3; matrix products, arithmetic and copies ran while one was open for 0% -> 2% of each run, Pallas kernels for 2% -> 3%
where the time goes in v3:
time: 189 us; the launch traced here: 188 us
  blocking collectives  75.2 us (40%)
  Pallas kernels  67.8 us (36%)
  waiting for transfers between devices  19.5 us (10%)
  starting transfers between devices  15 us (8%)
  local copies, waits for them, and re-layouts  8.72 us (5%)
    all_to_all x2, blocking collectives, exchange(): return lax.all_to_all(x, axes, split_axis=0, concat_axis=0, tiled=True)  75.2 us
    pallas_call x6, Pallas kernels, run(): pl.pallas_call(kernel, out_shape=[jax.ShapeDtypeStruct(s, f32) for s in s...  67.8 us
    all_to_all x1, waiting for transfers between devices, exchange(): return lax.all_to_all(x, axes, split_axis=0, concat_axis=0, tiled=True)  13.4 us
    all_to_all x1, starting transfers between devices, exchange(): return lax.all_to_all(x, axes, split_axis=0, concat_axis=0, tiled=True)  11.1 us
    unnamed x18, local copies, waits for them, and re-layouts  4.39 us
    ppermute x1, waiting for transfers between devices, body(): lax.ppermute(first_layer, 'line', [(i + 1, i) for i in range(RANGES - 1)])  4.16 us
  transfers between devices with their start and end apart: 3, of which 3 were waited for; matrix products, arithmetic and copies ran while one was open for 2% of the time, Pallas kernels for 3%

profile of v3, /device:TPU:0, one launch (start us, length us, event | category | flops | bytes accessed | tf_op | source)
XLA Modules:
  0.0 187.9 jit_solution(6926906153700038986)
XLA Ops:
  0.0 0.0 copy-start.2
  0.0 0.9 shift-right-arithmetic_multiply_fusion.offset_ref
  0.9 0.0 copy-start
  0.9 1.7 copy-done
  2.6 0.0 copy-start.3
  2.6 0.8 copy-done.3
  3.5 0.0 copy-start.4
  3.5 0.8 copy-done.4
  4.3 24.1 %shard_map.91 = (f32[128,8,128]{2,1,0:T(8,128)}, f32[8256,128]{1,0:T(8,128)}) custom-call(s32[128,128]{1,0:T(8,128)S(1)} %shift-right-arithmetic_multiply_fusion.offset_ref, s32[128,128]{1,0:T(8,128)S(1)} %bitcast.21, f32[128,128]{1,0:T(8,128)S(1)} %bitcast.22, f32[5120,128]{1,0:T(8,128)S(1)} %bitcast.16), custom_call_target="tpu_custom_call" | custom-call | tf_op jit(solution)/shard_map/pallas_call | solution.py:259
  28.4 11.1 %all-to-all-start = ((f32[128,8,128]{2,1,0:T(8,128)}), f32[128,8,128]{2,1,0:T(8,128)S(1)}, u32[]{:S(2)}, u32[]{:S(2)}) async-start(f32[128,8,128]{2,1,0:T(8,128)} %get-tuple-element.12), calls=%async_computation | async-start | bytes 1048576 | tf_op jit(solution)/shard_map/all_to_all | solution.py:324
  39.6 0.0 copy-done.2
  39.6 0.0 copy-start.6
  39.6 0.0 copy-start.7
  39.6 0.0 copy-start.5
  39.6 0.1 copy.16.offset_ref
  39.7 13.4 %all-to-all-done = f32[128,8,128]{2,1,0:T(8,128)S(1)} async-done(((f32[128,8,128]{2,1,0:T(8,128)}), f32[128,8,128]{2,1,0:T(8,128)S(1)}, u32[]{:S(2)}, u32[]{:S(2)}) %all-to-all-start) | async-done | bytes 524320 | tf_op jit(solution)/shard_map/all_to_all | solution.py:324
  53.2 27.2 %shard_map.92 = (f32[4,5,272,128]{3,2,1,0:T(8,128)S(1)}, f32[5,256,128]{2,1,0:T(8,128)}, f32[5,256,128]{2,1,0:T(8,128)}) custom-call(s32[128,128]{1,0:T(8,128)S(1)} %copy.16.offset_ref, s32[128,128]{1,0:T(8,128)S(1)} %bitcast.20, f32[1024,128]{1,0:T(8,128)S(1)} %bitcast.17, f32[8256,128]{1,0:T(8,128)} %get-tuple-element.13.kept_ref), custom_call_target="tpu_custom_call" | custom-call | tf_op jit(solution)/shard_map/pallas_call | solution.py:259
  80.4 2.6 %collective-permute-start = (f32[5,256,128]{2,1,0:T(8,128)}, f32[5,256,128]{2,1,0:T(8,128)S(1)}, u32[]{:S(2)}, u32[]{:S(2)}) collective-permute-start(f32[5,256,128]{2,1,0:T(8,128)} %get-tuple-element.15), channel_id=1, source_target_pairs={{0,1},{1,2},{2,3},{3,4},{4,5},{5,6},{6,7},{7,8},{8,9},{9,10},{10,1... | collective-permute-start | bytes 1966088 | tf_op jit(solution)/shard_map/ppermute | solution.py:342
  83.0 1.3 collective-permute-start.1
  84.3 0.0 copy-done.6
  84.3 0.0 copy-done.7
  85.0 0.0 copy-done.5
  85.0 1.1 reshape_squeeze.3
  86.1 2.1 %copy.21 = f32[4,16,4,16]{3,2,1,0:T(4,128)} copy(f32[4,16,4,16]{2,3,0,1:T(8,128)} %bitcast.23) | data formatting | bytes 32768 | tf_op jit(solution)/shard_map/transpose | solution.py:309
  88.2 1.0 reshape.20.inverse_ref
  89.3 0.0 copy-start.1
  89.3 0.9 copy-done.1
  90.2 5.2 %shard_map.93.middle_ref = f32[16,5,2,16,128]{4,3,2,1,0:T(8,128)S(1)} custom-call(f32[1,5,5]{2,1,0:T(8,128)S(1)} %copy.19.a_ref, f32[1,5,5]{2,1,0:T(8,128)S(1)} %copy.20.b_ref, f32[1]{0:T(128)S(6)} %copy.22.damp_ref, f32[4,5,272,128]{3,2,1,0:T(8,128)S(1)} %get-tuple-element.14.field_ref, f32[256,256]{1,0:T(8,128)S(1)} %bitcast.18), custom_call_target="tpu_custom_call" | custom-call | tf_op jit(solution)/shard_map/pallas_call | solution.py:259
  95.4 1.9 %collective-permute-done.low_ref = f32[5,256,128]{2,1,0:T(8,128)S(1)} collective-permute-done((f32[5,256,128]{2,1,0:T(8,128)}, f32[5,256,128]{2,1,0:T(8,128)S(1)}, u32[]{:S(2)}, u32[]{:S(2)}) %collective-permute-start) | collective-permute-done | bytes 655392 | tf_op jit(solution)/shard_map/ppermute | solution.py:342
  97.3 4.2 %collective-permute-done.1.high_ref = f32[5,256,128]{2,1,0:T(8,128)} collective-permute-done((f32[5,256,128]{2,1,0:T(8,128)}, f32[5,256,128]{2,1,0:T(8,128)}, u32[]{:S(2)}, u32[]{:S(2)}) %collective-permute-start.1) | collective-permute-done | bytes 655392 | tf_op jit(solution)/shard_map/ppermute | solution.py:343
  101.5 5.7 %shard_map.94 = f32[16,5,4,16,128]{4,3,2,1,0:T(8,128)S(1)} custom-call(f32[1,5,5]{2,1,0:T(8,128)S(1)} %copy.19.a_ref, f32[1,5,5]{2,1,0:T(8,128)S(1)} %copy.20.b_ref, f32[1]{0:T(128)S(6)} %copy.22.damp_ref, f32[4,5,272,128]{3,2,1,0:T(8,128)S(1)} %get-tuple-element.14.field_ref, f32[256,256]{1,0:T(8,128)S(1)} %bitcast.19, ...), custom_call_target="tpu_custom_call" | custom-call | tf_op jit(solution)/shard_map/pallas_call | solution.py:259
  107.2 40.1 %all_to_all.15 = f32[16,5,4,16,128]{4,3,2,1,0:T(8,128)S(1)} all-to-all(f32[16,5,4,16,128]{4,3,2,1,0:T(8,128)S(1)} %shard_map.94), channel_id=1, replica_groups=mesh['blk'=8,'line'=16] {'line'}, dimensions={0} | all-to-all | bytes 5242880 | tf_op jit(solution)/shard_map/all_to_all | solution.py:324
  147.3 3.7 %shard_map.95 = f32[5120,128]{1,0:T(8,128)S(1)} custom-call(f32[64,64]{1,0:T(8,128)S(1)} %reshape.20.inverse_ref, f32[5120,128]{1,0:T(8,128)S(1)} %bitcast.14), custom_call_target="tpu_custom_call" | custom-call | tf_op jit(solution)/shard_map/pallas_call | solution.py:259
  151.0 35.1 %all_to_all.16.back_ref = f32[16,5,4,16,128]{4,3,2,1,0:T(8,128)S(1)} all-to-all(f32[16,5,4,16,128]{4,3,2,1,0:T(8,128)S(1)} %bitcast.15), channel_id=1, replica_groups=mesh['blk'=8,'line'=16] {'line'}, dimensions={0} | all-to-all | bytes 5242880 | tf_op jit(solution)/shard_map/all_to_all | solution.py:324
  186.1 1.8 shard_map.96
  (3 shorter events, 0.0 us)
Async XLA Ops:
  0.0 39.6 %copy-start.2 = (s32[1,128,128]{2,1,0:T(8,128)S(1)}, s32[1,128,128]{2,1,0:T(8,128)}, u32[]{:S(2)}) copy-start(s32[1,128,128]{2,1,0:T(8,128)} %param.17) | copy-start | bytes 196612
  0.9 1.7 copy-start
  2.6 0.8 copy-start.3
  3.5 0.8 copy-start.4
  28.4 24.8 %all-to-all-start = ((f32[128,8,128]{2,1,0:T(8,128)}), f32[128,8,128]{2,1,0:T(8,128)S(1)}, u32[]{:S(2)}, u32[]{:S(2)}) async-start(f32[128,8,128]{2,1,0:T(8,128)} %get-tuple-element.12), calls=%async_computation | async-start | bytes 1048576 | tf_op jit(solution)/shard_map/all_to_all | solution.py:324
  39.6 44.7 %copy-start.6 = (f32[1,5,5]{2,0,1:T(1,128)S(1)}, f32[1,5,5]{2,0,1:T(1,128)}, u32[]{:S(2)}) copy-start(f32[1,5,5]{2,0,1:T(1,128)} %param.10) | copy-start | bytes 304
  39.6 44.7 %copy-start.7 = (f32[1,5,5]{2,0,1:T(1,128)S(1)}, f32[1,5,5]{2,0,1:T(1,128)}, u32[]{:S(2)}) copy-start(f32[1,5,5]{2,0,1:T(1,128)} %param.11) | copy-start | bytes 304
  39.6 45.4 %copy-start.5 = (f32[1,64,64]{2,1,0:T(8,128)S(1)}, f32[1,64,64]{2,1,0:T(8,128)}, u32[]{:S(2)}) copy-start(f32[1,64,64]{2,1,0:T(8,128)} %param.14) | copy-start | bytes 49156
  80.4 16.9 %collective-permute-start = (f32[5,256,128]{2,1,0:T(8,128)}, f32[5,256,128]{2,1,0:T(8,128)S(1)}, u32[]{:S(2)}, u32[]{:S(2)}) collective-permute-start(f32[5,256,128]{2,1,0:T(8,128)} %get-tuple-element.15), channel_id=1, source_target_pairs={{0,1},{1,2},{2,3},{3,4},{4,5},{5,6},{6,7},{7,8},{8,9},{9,10},{10,1... | collective-permute-start | bytes 1966088 | tf_op jit(solution)/shard_map/ppermute | solution.py:342
  83.0 18.5 %collective-permute-start.1 = (f32[5,256,128]{2,1,0:T(8,128)}, f32[5,256,128]{2,1,0:T(8,128)}, u32[]{:S(2)}, u32[]{:S(2)}) collective-permute-start(f32[5,256,128]{2,1,0:T(8,128)} %get-tuple-element.16), channel_id=1, source_target_pairs={{1,0},{2,1},{3,2},{4,3},{5,4},{6,5},{7,6},{8,7},{9,8},{10,9},{11,1... | collective-permute-start | bytes 1966088 | tf_op jit(solution)/shard_map/ppermute | solution.py:343
  89.3 1.0 copy-start.1

commit v4 on v3

v4 whole, which is shorter than its diff:
```python
import jax
import jax.numpy as jnp
from jax import lax
from jax.experimental import pallas as pl
from jax.experimental.pallas import tpu as pltpu
from jax.sharding import PartitionSpec as P

V, NI, CJ, NK, PIECES, SLOTS, RANGES = 5, 256, 4, 128, 128, 128, 16
ROWS = NI * CJ
PAD = CJ
DEPTH = (ROWS + 2 * PAD) * 8
CHUNK = NI // RANGES
SLAB = (CHUNK + 2) * CJ
NJ = CJ * RANGES
f32 = jnp.float32


def gather_kernel(offset_ref, lane_ref, weight_ref, st_ref, out_ref, kept_ref, tiles, want, mix, picked, sem):
    lane = lax.broadcasted_iota(jnp.int32, (8, 128), 1)
    sub = lax.broadcasted_iota(jnp.int32, (8, 128), 0)
    odd = lane & 1
    half = lane >> 1
    even = (lane * 2) & 127
    for t in range(PAD):
        tiles[t * 8 : t * 8 + 8, :] = jnp.zeros((8, 128), f32)

    def lay(b, carry):
        for t in range(2):
            c = b * 2 + t
            for v in range(V):
                tiles[pl.ds(PAD * 8 + c * 64 + v, 8, stride=8), :] = st_ref[
                    pl.ds(pl.multiple_of(v * ROWS + c * 8, 8), 8), :
                ]
        return carry

    lax.fori_loop(0, ROWS // 16, lay, 0)
    keep = pltpu.make_async_copy(tiles, kept_ref, sem)
    keep.start()

    def before(b, carry):
        for t in range(4):
            r = pl.ds(pl.multiple_of(b * 32 + t * 8, 8), 8)
            cells = lane_ref[r, :] & 127
            weights = weight_ref[r, :]
            for h in range(2):
                want[h, r, :] = jnp.take_along_axis(cells, half + 64 * h, axis=1) + odd
                w = jnp.take_along_axis(weights, half + 64 * h, axis=1)
                mix[h, r, :] = jnp.where(odd == 0, w, 1.0 - w)
        return carry

    lax.fori_loop(0, PIECES // 32, before, 0)

    def piece(m, carry):
        for h in range(2):
            index = jnp.broadcast_to(want[h, pl.ds(m, 1), :], (8, 128))
            acc = jnp.zeros((8, 128), f32)
            for q in range(64):
                x = tiles[pl.ds(pl.multiple_of(offset_ref[m, 64 * h + q], 8), 8), :]
                acc = jnp.where(half == q, jnp.take_along_axis(x, index, axis=1), acc)
            picked[m, h] = acc * jnp.broadcast_to(mix[h, pl.ds(m, 1), :], (8, 128))
        return carry

    lax.fori_loop(0, PIECES, piece, 0, unroll=8)

    def after(b, carry):
        for t in range(16):
            sums = []
            for h in range(2):
                x = picked[b * 16 + t, h]
                x = x + pltpu.roll(x, 127, axis=1)
                sums.append(jnp.take_along_axis(x, even, axis=1))
            x = jnp.where(lane < 64, sums[0], sums[1])
            out_ref[b * 16 + t] = jnp.where(sub < V, x, 0.0)
        return carry

    lax.fori_loop(0, PIECES // 16, after, 0)
    keep.wait()


def scatter_kernel(offset_ref, cell_ref, arrived_ref, kept_ref, send_ref, tiles, parts, ping, pong, sem):
    keep = pltpu.make_async_copy(kept_ref, tiles, sem)
    keep.start()
    sub = lax.broadcasted_iota(jnp.int32, (8, 128), 0)

    def build(b, carry):
        r = pl.ds(pl.multiple_of(b * 16, 16), 16)
        x = []
        for t in range(2):
            lanes = (cell_ref[pl.ds(2 * b + t, 1), :] & 127).astype(f32)
            values = arrived_ref[pl.ds(pl.multiple_of(b * 16 + t * 8, 8), 8), :]
            x.append(jnp.where(sub == V, jnp.broadcast_to(lanes, (8, 128)), values))
        x = jnp.concatenate(x, axis=0)
        coarse = x.astype(jnp.bfloat16)
        parts[r, 0:128] = coarse
        parts[r, 128:256] = (x - coarse.astype(f32)).astype(jnp.bfloat16)
        return carry

    lax.fori_loop(0, PIECES // 2, build, 0, unroll=4)
    lane = lax.broadcasted_iota(jnp.int32, (8, 128), 1).astype(f32)
    square = (2 * SLOTS, 2 * NK)
    code = (lax.broadcasted_iota(jnp.int32, square, 0) & 127) - (lax.broadcasted_iota(jnp.int32, square, 1) >> 7)
    group = PIECES // 4

    def ones(pair):
        return jnp.where(code == 2 * pair, 1.0, 0.0).astype(jnp.bfloat16)

    def spread(mask, buffer, g):
        rows = slice(g * group * 8, (g + 1) * group * 8)
        buffer[rows, :] = jnp.dot(parts[rows, :], mask, preferred_element_type=f32)

    def put(pair, buffer, g):
        for n in range(g * group, (g + 1) * group):
            for c in range(2):
                columns = slice(c * 128, c * 128 + 128)
                offset = pl.multiple_of(offset_ref[2 * pair + c, n], 8)
                value = buffer[n * 8 : n * 8 + 8, columns]
                lanes = jnp.broadcast_to(buffer[n * 8 + V : n * 8 + V + 1, columns], (8, 128))
                pltpu.store(tiles.at[pl.ds(offset, 8), :], value, mask=lane == lanes)

    def step(pair, now, later):
        mask = ones(pair + 1)
        for g in range(4):
            spread(mask, later, g)
            put(pair, now, g)

    first = ones(0)
    for g in range(4):
        spread(first, ping, g)
    keep.wait()

    def both(i, carry):
        step(2 * i, ping, pong)
        step(2 * i + 1, pong, ping)
        return carry

    lax.fori_loop(0, SLOTS // 4, both, 0)
    for t in range(PAD):
        tiles[(PAD + ROWS + t) * 8 : (PAD + ROWS + t + 1) * 8, :] = jnp.zeros((8, 128), f32)

    def slab(c, carry):
        for v in range(V):
            for t in range(0, SLAB, 8):
                send_ref[pl.ds(pl.multiple_of((c * V + v) * SLAB + t, 8), 8), :] = tiles[
                    pl.ds((c * CHUNK * CJ + t) * 8 + v, 8, stride=8), :
                ]
        return carry

    lax.fori_loop(0, RANGES, slab, 0)


def halves(x):
    coarse = x.astype(jnp.bfloat16)
    return coarse, (x - coarse.astype(f32)).astype(jnp.bfloat16)


def product(x, y):
    def dot(p, q):
        return jnp.dot(p, q, preferred_element_type=f32)

    return dot(x[0], y[0]) + (dot(x[0], y[1]) + dot(x[1], y[0]))


def slab_kernel(a_ref, b_ref, damp_ref, inverse_ref, in_ref, out_ref, rhs, coarse, fine):
    lane = lax.broadcasted_iota(jnp.int32, (CHUNK, 128), 1)
    damp = damp_ref[0]
    a = [[0.5 * a_ref[0, u, v] for v in range(V)] for u in range(V)]
    b = [[0.5 * b_ref[0, u, v] for v in range(V)] for u in range(V)]

    def one(s, carry):
        def cells(s, v, di, j):
            return in_ref[pl.ds((s * V + v) * SLAB + (1 + di) * CJ + j, CHUNK, stride=CJ), :]

        for j in range(CJ):
            di, dj, lap = [], [], []
            for v in range(V):
                c = cells(s, v, 0, j)
                im = cells(s, v, -1, j)
                ip = cells(s, v, 1, j)
                if j == 0:
                    jm = jnp.where(s > 0, cells(jnp.maximum(s - 1, 0), v, 0, CJ - 1), 0.0)
                else:
                    jm = cells(s, v, 0, j - 1)
                if j == CJ - 1:
                    jp = jnp.where(s < RANGES - 1, cells(jnp.minimum(s + 1, RANGES - 1), v, 0, 0), 0.0)
                else:
                    jp = cells(s, v, 0, j + 1)
                kp = jnp.where(lane == NK - 1, 0.0, pltpu.roll(c, NK - 1, axis=1))
                km = jnp.where(lane == 0, 0.0, pltpu.roll(c, 1, axis=1))
                lap.append(ip + im + jp + jm + kp + km - 6.0 * c)
                di.append(ip - im)
                dj.append(jp - jm)
            for u in range(V):
                r = damp * lap[u]
                for v in range(V):
                    r = r - (a[u][v] * di[v] + b[u][v] * dj[v])
                rhs[u, pl.ds(pl.multiple_of((s * CJ + j) * CHUNK, CHUNK), CHUNK), :] = r
        return carry

    lax.fori_loop(0, RANGES, one, 0)
    matrix = halves(jnp.concatenate([inverse_ref[pl.ds(j, RANGES, stride=CJ), :] for j in range(CJ)], axis=0))
    step = V * CJ * CHUNK
    for u in range(V):
        for i in range(CHUNK):
            columns = slice(i * NK, (i + 1) * NK)
            coarse[:, columns], fine[:, columns] = halves(rhs[u, pl.ds(i, NJ, stride=CHUNK), :])
        solved = product(matrix, (coarse[...], fine[...]))
        for j in range(CJ):
            for i in range(CHUNK):
                for s in range(0, RANGES, 8):
                    start = s * step + (u * CJ + j) * CHUNK + i
                    out_ref[pl.ds(start, 8, stride=step), :] = solved[
                        j * RANGES + s : j * RANGES + s + 8, i * NK : (i + 1) * NK
                    ]


def final_kernel(inverse_ref, send_ref, back_ref, out_ref):
    matrix = halves(inverse_ref[...])
    for v in range(V):
        lines = jnp.concatenate([back_ref[:, v, j].reshape(NI, NK) for j in range(CJ)], axis=1)
        solved = product(matrix, halves(lines))
        for j in range(CJ):
            for c in range(RANGES):
                x = send_ref[pl.ds((c * V + v) * SLAB + CJ + j, CHUNK, stride=CJ), :]
                out_ref[pl.ds(v * ROWS + c * CHUNK * CJ + j, CHUNK, stride=CJ), :] = (
                    x + solved[c * CHUNK : (c + 1) * CHUNK, j * NK : (j + 1) * NK]
                )


smem = pl.BlockSpec(memory_space=pltpu.SMEM)
vmem = pl.BlockSpec(memory_space=pltpu.VMEM)
hbm = pl.BlockSpec(memory_space=pltpu.HBM)


def run(kernel, specs, shapes, scratch, limit, *args, outs=None, sems=0):
    one = not isinstance(shapes, list)
    shapes = [shapes] if one else shapes
    out = pl.pallas_call(
        kernel,
        out_shape=[jax.ShapeDtypeStruct(s, f32) for s in shapes],
        in_specs=specs,
        out_specs=outs or [vmem] * len(shapes),
        scratch_shapes=[pltpu.VMEM(s, t) for s, t in scratch] + [pltpu.SemaphoreType.DMA] * sems,
        compiler_params=pltpu.CompilerParams(vmem_limit_bytes=limit << 20),
    )(*args)
    return out[0] if one else out


def offsets_of(cells):
    return ((cells >> 7) + PAD) * 8


def gather_call(cells, weights, st):
    scratch = [((DEPTH, NK), f32), ((2, PIECES, NK), jnp.int32), ((2, PIECES, NK), f32), ((PIECES, 2, 8, NK), f32)]
    shapes = [(PIECES, 8, SLOTS), (DEPTH, NK)]
    specs = [smem, vmem, vmem, vmem]
    args = (offsets_of(cells), cells, weights, st)
    return run(gather_kernel, specs, shapes, scratch, 48, *args, outs=[vmem, hbm], sems=1)


def scatter_call(cells, arrived, kept):
    wide = (PIECES * 8, 2 * NK)
    return run(
        scatter_kernel,
        [smem, vmem, vmem, hbm],
        (RANGES * V * SLAB, NK),
        [((DEPTH, NK), f32), (wide, jnp.bfloat16), (wide, f32), (wide, f32)],
        48,
        offsets_of(cells).T,
        cells,
        arrived.reshape(PIECES * 8, NK),
        kept,
        sems=1,
    )


def slab_call(a, b, damp, inverse, lines):
    wide = ((NJ, CHUNK * NK), jnp.bfloat16)
    return run(
        slab_kernel,
        [smem, smem, smem, vmem, vmem],
        (RANGES * V * CJ * CHUNK, NK),
        [((V, NJ * CHUNK, NK), f32), wide, wide],
        20,
        a,
        b,
        damp,
        inverse,
        lines,
    )


def final_call(inverse, send, back):
    back = back.reshape(RANGES, V, CJ, CHUNK, NK)
    return run(final_kernel, [vmem] * 3, (V * ROWS, NK), [], 20, inverse, send, back)


def exchange(x, axes):
    return lax.all_to_all(x, axes, split_axis=0, concat_axis=0, tiled=True)


def body(
    state,
    first_flux,
    second_flux,
    viscosity,
    first_inverse,
    second_inverse,
    donor_cell,
    donor_weight,
    receptor_cell,
):
    st = state.reshape(V * ROWS, NK)
    donated, kept = gather_call(donor_cell[0], donor_weight[0], st)
    arrived = exchange(donated, ("blk", "line"))
    send = scatter_call(receptor_cell[0], arrived, kept)
    lines = exchange(send, "line")
    back = exchange(slab_call(first_flux, second_flux, viscosity, second_inverse[0], lines), "line")
    return final_call(first_inverse[0], send, back).reshape(1, V, NI, CJ, NK)


def solution(mesh):
    in_specs = (
        P("blk", None, None, "line", None),
        P("blk", None, None),
        P("blk", None, None),
        P("blk"),
        P("blk", None, None),
        P("blk", None, None),
        P(("blk", "line"), None, None),
        P(("blk", "line"), None, None),
        P(("blk", "line"), None, None),
    )
    out_specs = P("blk", None, None, "line", None)
    return jax.shard_map(body, mesh=mesh, in_specs=in_specs, out_specs=out_specs, check_vma=False)
```

time: 189 us -> 179 us (0.947)
  waiting for transfers between devices: 19.5 us -> 58.3 us
  blocking collectives: 75.2 us -> 37.9 us
  Pallas kernels: 67.8 us -> 62.6 us
  local copies, waits for them, and re-layouts: 8.72 us -> 3.54 us
    all_to_all x1 -> x2, waiting for transfers between devices: 13.4 us -> 58.3 us  [exchange(): return lax.all_to_all(x, axes, split_axis=0, concat_axis=0, tiled=True)]
    all_to_all x2 -> x1, blocking collectives: 75.2 us -> 37.9 us  [exchange(): return lax.all_to_all(x, axes, split_axis=0, concat_axis=0, tiled=True)]
    ppermute x2 -> x0, waiting for transfers between devices: 6.06 us -> none  [the longest x1 4.16 us: body(): lax.ppermute(first_layer, 'line', [(i + 1, i) for i in range(RANGES - 1)])]
    pallas_call x6 -> x4, Pallas kernels: 67.8 us -> 62.6 us  [run(): pl.pallas_call(kernel, out_shape=[jax.ShapeDtypeStruct(s, f32) for s in s...]
    all_to_all x1 -> x2, starting transfers between devices: 11.1 us -> 15 us  [exchange(): return lax.all_to_all(x, axes, split_axis=0, concat_axis=0, tiled=True)]
    ppermute x2 -> x0, starting transfers between devices: 3.86 us -> none  [the longest x1 2.57 us: body(): lax.ppermute(last_layer, 'line', [(i, i + 1) for i in range(RANGES - 1)])]
    transpose x1 -> x0, local copies, waits for them, and re-layouts: 2.13 us -> none  [ordered(): inverse.reshape(RANGES, CJ, RANGES, CJ).transpose(1, 0, 3, 2)]
  transfers between devices with their start and end apart: 3 -> 2, of which waited for: 3 -> 2; matrix products, arithmetic and copies ran while one was open for 2% -> 0% of each run, Pallas kernels for 3% -> 0%
where the time goes in v4:
time: 179 us
  Pallas kernels  62.6 us (35%)
  waiting for transfers between devices  58.3 us (33%)
  blocking collectives  37.9 us (21%)
  starting transfers between devices  15 us (8%)
  local copies, waits for them, and re-layouts  3.54 us (2%)
    pallas_call x4, Pallas kernels, run(): pl.pallas_call(kernel, out_shape=[jax.ShapeDtypeStruct(s, f32) for s in s...  62.6 us
    all_to_all x2, waiting for transfers between devices, exchange(): return lax.all_to_all(x, axes, split_axis=0, concat_axis=0, tiled=True)  58.3 us
    all_to_all x1, blocking collectives, exchange(): return lax.all_to_all(x, axes, split_axis=0, concat_axis=0, tiled=True)  37.9 us
    all_to_all x2, starting transfers between devices, exchange(): return lax.all_to_all(x, axes, split_axis=0, concat_axis=0, tiled=True)  15 us
  transfers between devices with their start and end apart: 2, of which 2 were waited for; matrix products, arithmetic and copies ran while one was open for 0% of the time, Pallas kernels for 0%

profile of v4, /device:TPU:0, one launch (start us, length us, event | category | flops | bytes accessed | tf_op | source)
XLA Modules:
  0.0 179.0 jit_solution(10228411570105243578)
XLA Ops:
  0.0 0.0 copy-start.1
  0.0 0.9 add_multiply_fusion.offset_ref
  0.9 0.0 copy-start
  0.9 1.7 copy-done
  2.6 0.0 copy-start.3
  2.6 0.8 copy-done.3
  3.5 0.0 copy-start.4
  3.5 0.8 copy-done.4
  4.3 23.9 %shard_map.91 = (f32[128,8,128]{2,1,0:T(8,128)}, f32[8256,128]{1,0:T(8,128)}) custom-call(s32[128,128]{1,0:T(8,128)S(1)} %add_multiply_fusion.offset_ref, s32[128,128]{1,0:T(8,128)S(1)} %bitcast.23, f32[128,128]{1,0:T(8,128)S(1)} %bitcast.24, f32[5120,128]{1,0:T(8,128)S(1)} %bitcast.19), custom_call_target="tpu_custom_call" | custom-call | tf_op jit(solution)/shard_map/pallas_call | solution.py:237
  28.3 11.1 %all-to-all-start = ((f32[128,8,128]{2,1,0:T(8,128)}), f32[128,8,128]{2,1,0:T(8,128)S(1)}, u32[]{:S(2)}, u32[]{:S(2)}) async-start(f32[128,8,128]{2,1,0:T(8,128)} %get-tuple-element.7), calls=%async_computation | async-start | bytes 1048576 | tf_op jit(solution)/shard_map/all_to_all | solution.py:298
  39.4 0.0 copy-done.1
  39.4 0.1 copy.10.offset_ref
  39.5 13.5 %all-to-all-done = f32[128,8,128]{2,1,0:T(8,128)S(1)} async-done(((f32[128,8,128]{2,1,0:T(8,128)}), f32[128,8,128]{2,1,0:T(8,128)S(1)}, u32[]{:S(2)}, u32[]{:S(2)}) %all-to-all-start) | async-done | bytes 524320 | tf_op jit(solution)/shard_map/all_to_all | solution.py:298
  53.0 26.7 %shard_map.92.send_ref = f32[5760,128]{1,0:T(8,128)} custom-call(s32[128,128]{1,0:T(8,128)S(1)} %copy.10.offset_ref, s32[128,128]{1,0:T(8,128)S(1)} %bitcast.21, f32[1024,128]{1,0:T(8,128)S(1)} %bitcast.20, f32[8256,128]{1,0:T(8,128)} %get-tuple-element.8.kept_ref), custom_call_target="tpu_custom_call" | custom-call | tf_op jit(solution)/shard_map/pallas_call | solution.py:237
  79.8 0.0 copy-start.6
  79.8 0.0 copy-start.7
  79.8 0.0 copy-start.5
  79.8 3.9 %all-to-all-start.1 = ((f32[16,360,128]{2,1,0:T(8,128)}), f32[16,360,128]{2,1,0:T(8,128)S(1)}, u32[]{:S(2)}, u32[]{:S(2)}) async-start(f32[16,360,128]{2,1,0:T(8,128)} %bitcast.8), calls=%async_computation.1 | async-start | bytes 5898240 | tf_op jit(solution)/shard_map/all_to_all | solution.py:298
  84.3 0.0 copy-done.6
  84.4 0.0 copy-done.7
  84.4 44.8 %all-to-all-done.1 = f32[16,360,128]{2,1,0:T(8,128)S(1)} async-done(((f32[16,360,128]{2,1,0:T(8,128)}), f32[16,360,128]{2,1,0:T(8,128)S(1)}, u32[]{:S(2)}, u32[]{:S(2)}) %all-to-all-start.1) | async-done | bytes 2949152 | tf_op jit(solution)/shard_map/all_to_all | solution.py:298
  129.2 0.0 copy-done.5
  129.2 7.3 %shard_map.93 = f32[5120,128]{1,0:T(8,128)S(1)} custom-call(f32[1,5,5]{2,1,0:T(8,128)S(1)} %copy.11.a_ref, f32[1,5,5]{2,1,0:T(8,128)S(1)} %copy.12.b_ref, f32[1]{0:T(128)S(6)} %copy.13.damp_ref, f32[64,64]{1,0:T(8,128)S(1)} %bitcast.25, f32[5760,128]{1,0:T(8,128)S(1)} %bitcast.16), custom_call_target="tpu_custom_call" | custom-call | tf_op jit(solution)/shard_map/pallas_call | solution.py:237
  136.5 0.0 copy-start.2
  136.5 37.9 %all_to_all.25 = f32[16,320,128]{2,1,0:T(8,128)S(1)} all-to-all(f32[16,320,128]{2,1,0:T(8,128)S(1)} %bitcast.17), channel_id=1, replica_groups=mesh['blk'=8,'line'=16] {'line'}, dimensions={0} | all-to-all | bytes 5242880 | tf_op jit(solution)/shard_map/all_to_all | solution.py:298
  174.4 0.0 copy-done.2
  174.4 4.5 %shard_map.94 = f32[5120,128]{1,0:T(8,128)} custom-call(f32[256,256]{1,0:T(8,128)S(1)} %bitcast.22, f32[5760,128]{1,0:T(8,128)} %shard_map.92.send_ref, f32[16,5,4,16,128]{4,3,2,1,0:T(8,128)S(1)} %bitcast.18), custom_call_target="tpu_custom_call" | custom-call | tf_op jit(solution)/shard_map/pallas_call | solution.py:237
  (3 shorter events, 0.0 us)
Async XLA Ops:
  0.0 39.4 %copy-start.1 = (s32[1,128,128]{2,1,0:T(8,128)S(1)}, s32[1,128,128]{2,1,0:T(8,128)}, u32[]{:S(2)}) copy-start(s32[1,128,128]{2,1,0:T(8,128)} %param.17) | copy-start | bytes 196612
  0.9 1.7 copy-start
  2.6 0.8 copy-start.3
  3.5 0.8 copy-start.4
  28.3 24.8 %all-to-all-start = ((f32[128,8,128]{2,1,0:T(8,128)}), f32[128,8,128]{2,1,0:T(8,128)S(1)}, u32[]{:S(2)}, u32[]{:S(2)}) async-start(f32[128,8,128]{2,1,0:T(8,128)} %get-tuple-element.7), calls=%async_computation | async-start | bytes 1048576 | tf_op jit(solution)/shard_map/all_to_all | solution.py:298
  79.8 4.6 %copy-start.6 = (f32[1,5,5]{2,0,1:T(1,128)S(1)}, f32[1,5,5]{2,0,1:T(1,128)}, u32[]{:S(2)}) copy-start(f32[1,5,5]{2,0,1:T(1,128)} %param.10) | copy-start | bytes 304
  79.8 4.6 %copy-start.7 = (f32[1,5,5]{2,0,1:T(1,128)S(1)}, f32[1,5,5]{2,0,1:T(1,128)}, u32[]{:S(2)}) copy-start(f32[1,5,5]{2,0,1:T(1,128)} %param.11) | copy-start | bytes 304
  79.8 49.4 %copy-start.5 = (f32[1,64,64]{2,1,0:T(8,128)S(1)}, f32[1,64,64]{2,1,0:T(8,128)}, u32[]{:S(2)}) copy-start(f32[1,64,64]{2,1,0:T(8,128)} %param.14) | copy-start | bytes 49156
  79.8 49.4 %all-to-all-start.1 = ((f32[16,360,128]{2,1,0:T(8,128)}), f32[16,360,128]{2,1,0:T(8,128)S(1)}, u32[]{:S(2)}, u32[]{:S(2)}) async-start(f32[16,360,128]{2,1,0:T(8,128)} %bitcast.8), calls=%async_computation.1 | async-start | bytes 5898240 | tf_op jit(solution)/shard_map/all_to_all | solution.py:298
  136.5 37.9 %copy-start.2 = (f32[1,256,256]{2,1,0:T(8,128)S(1)}, f32[1,256,256]{2,1,0:T(8,128)}, u32[]{:S(2)}) copy-start(f32[1,256,256]{2,1,0:T(8,128)} %param.13) | copy-start | bytes 786436

commit v5 on v4

--- a/solution.py
+++ b/solution.py
@@ -15,27 +15,29 @@
 f32 = jnp.float32
 
 
-def gather_kernel(offset_ref, lane_ref, weight_ref, st_ref, out_ref, kept_ref, tiles, want, mix, picked, sem):
+def others(block, n):
+    return n + jnp.where(n >= block * RANGES, RANGES, 0)
+
+
+def gather_kernel(cell_hbm, weight_hbm, st_hbm, out_ref, kept_ref, lane_ref, weight_ref, st_ref, offset_vmem, tiles, want, mix, picked, offset_ref, sems):
+    copies = [
+        pltpu.make_async_copy(cell_hbm, lane_ref, sems.at[0]),
+        pltpu.make_async_copy(weight_hbm, weight_ref, sems.at[1]),
+        pltpu.make_async_copy(st_hbm, st_ref, sems.at[2]),
+    ]
+    for copy in copies:
+        copy.start()
+    block = lax.axis_index("blk")
     lane = lax.broadcasted_iota(jnp.int32, (8, 128), 1)
     sub = lax.broadcasted_iota(jnp.int32, (8, 128), 0)
     odd = lane & 1
     half = lane >> 1
     even = (lane * 2) & 127
-    for t in range(PAD):
-        tiles[t * 8 : t * 8 + 8, :] = jnp.zeros((8, 128), f32)
-
-    def lay(b, carry):
-        for t in range(2):
-            c = b * 2 + t
-            for v in range(V):
-                tiles[pl.ds(PAD * 8 + c * 64 + v, 8, stride=8), :] = st_ref[
-                    pl.ds(pl.multiple_of(v * ROWS + c * 8, 8), 8), :
-                ]
-        return carry
-
-    lax.fori_loop(0, ROWS // 16, lay, 0)
-    keep = pltpu.make_async_copy(tiles, kept_ref, sem)
-    keep.start()
+    copies[0].wait()
+    offset_vmem[...] = ((lane_ref[...] >> 7) + PAD) * 8
+    offsets = pltpu.make_async_copy(offset_vmem, offset_ref, sems.at[0])
+    offsets.start()
+    copies[1].wait()
 
     def before(b, carry):
         for t in range(4):
@@ -50,7 +52,34 @@
 
     lax.fori_loop(0, PIECES // 32, before, 0)
 
-    def piece(m, carry):
+    copies[2].wait()
+    for t in range(PAD):
+        tiles[t * 8 : t * 8 + 8, :] = jnp.zeros((8, 128), f32)
+        tiles[DEPTH - t * 8 - 8 : DEPTH - t * 8, :] = jnp.zeros((8, 128), f32)
+
+    def lay(b, carry):
+        for t in range(2):
+            c = b * 2 + t
+            for v in range(V):
+                tiles[pl.ds(PAD * 8 + c * 64 + v, 8, stride=8), :] = st_ref[
+                    pl.ds(pl.multiple_of(v * ROWS + c * 8, 8), 8), :
+                ]
+        return carry
+
+    lax.fori_loop(0, ROWS // 16, lay, 0)
+    keep = pltpu.make_async_copy(tiles, kept_ref, sems.at[2])
+    keep.start()
+    offsets.wait()
+
+    def own(m, carry):
+        for h in range(2):
+            picked[block * RANGES + m, h] = jnp.zeros((8, 128), f32)
+        return carry
+
+    lax.fori_loop(0, RANGES, own, 0)
+
+    def piece(k, carry):
+        m = others(block, k)
         for h in range(2):
             index = jnp.broadcast_to(want[h, pl.ds(m, 1), :], (8, 128))
             acc = jnp.zeros((8, 128), f32)
@@ -60,7 +89,7 @@
             picked[m, h] = acc * jnp.broadcast_to(mix[h, pl.ds(m, 1), :], (8, 128))
         return carry
 
-    lax.fori_loop(0, PIECES, piece, 0, unroll=8)
+    lax.fori_loop(0, PIECES - RANGES, piece, 0, unroll=8)
 
     def after(b, carry):
         for t in range(16):
@@ -70,14 +99,16 @@
                 x = x + pltpu.roll(x, 127, axis=1)
                 sums.append(jnp.take_along_axis(x, even, axis=1))
             x = jnp.where(lane < 64, sums[0], sums[1])
-            out_ref[b * 16 + t] = jnp.where(sub < V, x, 0.0)
+            for v in range(V):
+                out_ref[b * 16 + t, :, v * SLOTS : (v + 1) * SLOTS] = x[v : v + 1]
         return carry
 
     lax.fori_loop(0, PIECES // 16, after, 0)
     keep.wait()
 
 
-def scatter_kernel(offset_ref, cell_ref, arrived_ref, kept_ref, send_ref, tiles, parts, ping, pong, sem):
+def scatter_kernel(offset_ref, a_ref, b_ref, damp_ref, cell_ref, arrived_ref, kept_ref, send_ref, factor_ref, tiles, parts, ping, pong, sem):
+    block = lax.axis_index("blk")
     keep = pltpu.make_async_copy(kept_ref, tiles, sem)
     keep.start()
     sub = lax.broadcasted_iota(jnp.int32, (8, 128), 0)
@@ -86,20 +117,30 @@
         r = pl.ds(pl.multiple_of(b * 16, 16), 16)
         x = []
         for t in range(2):
-            lanes = (cell_ref[pl.ds(2 * b + t, 1), :] & 127).astype(f32)
-            values = arrived_ref[pl.ds(pl.multiple_of(b * 16 + t * 8, 8), 8), :]
-            x.append(jnp.where(sub == V, jnp.broadcast_to(lanes, (8, 128)), values))
+            n = others(block, 2 * b + t)
+            lanes = (cell_ref[pl.ds(n, 1), :] & 127).astype(f32)
+            values = jnp.broadcast_to(lanes, (8, 128))
+            for v in range(V):
+                row = arrived_ref[n, :, v * SLOTS : (v + 1) * SLOTS]
+                values = jnp.where(sub == v, jnp.broadcast_to(row, (8, 128)), values)
+            x.append(values)
         x = jnp.concatenate(x, axis=0)
         coarse = x.astype(jnp.bfloat16)
         parts[r, 0:128] = coarse
         parts[r, 128:256] = (x - coarse.astype(f32)).astype(jnp.bfloat16)
         return carry
 
-    lax.fori_loop(0, PIECES // 2, build, 0, unroll=4)
+    lax.fori_loop(0, (PIECES - RANGES) // 2, build, 0, unroll=4)
+    for u in range(V):
+        for v in range(V):
+            factor_ref[u * V + v : u * V + v + 1, :] = jnp.full((1, 128), 0.5 * a_ref[0, u, v], f32)
+            factor_ref[25 + u * V + v : 26 + u * V + v, :] = jnp.full((1, 128), 0.5 * b_ref[0, u, v], f32)
+    factor_ref[50:51, :] = jnp.full((1, 128), damp_ref[0], f32)
+    factor_ref[51:56, :] = jnp.zeros((5, 128), f32)
     lane = lax.broadcasted_iota(jnp.int32, (8, 128), 1).astype(f32)
     square = (2 * SLOTS, 2 * NK)
     code = (lax.broadcasted_iota(jnp.int32, square, 0) & 127) - (lax.broadcasted_iota(jnp.int32, square, 1) >> 7)
-    group = PIECES // 4
+    group = (PIECES - RANGES) // 4
 
     def ones(pair):
         return jnp.where(code == 2 * pair, 1.0, 0.0).astype(jnp.bfloat16)
@@ -160,11 +201,11 @@
     return dot(x[0], y[0]) + (dot(x[0], y[1]) + dot(x[1], y[0]))
 
 
-def slab_kernel(a_ref, b_ref, damp_ref, inverse_ref, in_ref, out_ref, rhs, coarse, fine):
+def slab_kernel(factor_ref, inverse_ref, in_ref, out_ref, rhs, coarse, fine):
     lane = lax.broadcasted_iota(jnp.int32, (CHUNK, 128), 1)
-    damp = damp_ref[0]
-    a = [[0.5 * a_ref[0, u, v] for v in range(V)] for u in range(V)]
-    b = [[0.5 * b_ref[0, u, v] for v in range(V)] for u in range(V)]
+
+    def factor(r):
+        return jnp.broadcast_to(factor_ref[r : r + 1, :], (CHUNK, 128))
 
     def one(s, carry):
         def cells(s, v, di, j):
@@ -190,9 +231,9 @@
                 di.append(ip - im)
                 dj.append(jp - jm)
             for u in range(V):
-                r = damp * lap[u]
+                r = factor(50) * lap[u]
                 for v in range(V):
-                    r = r - (a[u][v] * di[v] + b[u][v] * dj[v])
+                    r = r - (factor(u * V + v) * di[v] + factor(25 + u * V + v) * dj[v])
                 rhs[u, pl.ds(pl.multiple_of((s * CJ + j) * CHUNK, CHUNK), CHUNK), :] = r
         return carry
 
@@ -213,17 +254,27 @@
                     ]
 
 
-def final_kernel(inverse_ref, send_ref, back_ref, out_ref):
+def final_kernel(inverse_ref, send_hbm, back_ref, out_hbm, send_ref, out_ref, sems):
+    bring = pltpu.make_async_copy(send_hbm, send_ref, sems.at[V])
+    bring.start()
     matrix = halves(inverse_ref[...])
+    copies = []
     for v in range(V):
         lines = jnp.concatenate([back_ref[:, v, j].reshape(NI, NK) for j in range(CJ)], axis=1)
         solved = product(matrix, halves(lines))
+        if v == 0:
+            bring.wait()
         for j in range(CJ):
             for c in range(RANGES):
                 x = send_ref[pl.ds((c * V + v) * SLAB + CJ + j, CHUNK, stride=CJ), :]
                 out_ref[pl.ds(v * ROWS + c * CHUNK * CJ + j, CHUNK, stride=CJ), :] = (
                     x + solved[c * CHUNK : (c + 1) * CHUNK, j * NK : (j + 1) * NK]
                 )
+        rows = pl.ds(v * ROWS, ROWS)
+        copies.append(pltpu.make_async_copy(out_ref.at[rows, :], out_hbm.at[rows, :], sems.at[v]))
+        copies[-1].start()
+    for copy in copies:
+        copy.wait()
 
 
 smem = pl.BlockSpec(memory_space=pltpu.SMEM)
@@ -231,7 +282,7 @@
 hbm = pl.BlockSpec(memory_space=pltpu.HBM)
 
 
-def run(kernel, specs, shapes, scratch, limit, *args, outs=None, sems=0):
+def run(kernel, specs, shapes, scratch, limit, *args, outs=None, more=None):
     one = not isinstance(shapes, list)
     shapes = [shapes] if one else shapes
     out = pl.pallas_call(
@@ -239,59 +290,56 @@
         out_shape=[jax.ShapeDtypeStruct(s, f32) for s in shapes],
         in_specs=specs,
         out_specs=outs or [vmem] * len(shapes),
-        scratch_shapes=[pltpu.VMEM(s, t) for s, t in scratch] + [pltpu.SemaphoreType.DMA] * sems,
+        scratch_shapes=[pltpu.VMEM(s, t) for s, t in scratch] + (more or []),
         compiler_params=pltpu.CompilerParams(vmem_limit_bytes=limit << 20),
     )(*args)
     return out[0] if one else out
 
 
-def offsets_of(cells):
-    return ((cells >> 7) + PAD) * 8
+LANES = ((PIECES, SLOTS), jnp.int32)
 
 
 def gather_call(cells, weights, st):
-    scratch = [((DEPTH, NK), f32), ((2, PIECES, NK), jnp.int32), ((2, PIECES, NK), f32), ((PIECES, 2, 8, NK), f32)]
-    shapes = [(PIECES, 8, SLOTS), (DEPTH, NK)]
-    specs = [smem, vmem, vmem, vmem]
-    args = (offsets_of(cells), cells, weights, st)
-    return run(gather_kernel, specs, shapes, scratch, 48, *args, outs=[vmem, hbm], sems=1)
-
-
-def scatter_call(cells, arrived, kept):
-    wide = (PIECES * 8, 2 * NK)
+    scratch = [LANES, ((PIECES, SLOTS), f32), ((V * ROWS, NK), f32), LANES, ((DEPTH, NK), f32)]
+    scratch += [((2, PIECES, NK), jnp.int32), ((2, PIECES, NK), f32), ((PIECES, 2, 8, NK), f32)]
+    more = [pltpu.SMEM((PIECES, SLOTS), jnp.int32), pltpu.SemaphoreType.DMA((3,))]
+    shapes = [(PIECES, 1, V * SLOTS), (DEPTH, NK)]
+    return run(gather_kernel, [hbm] * 3, shapes, scratch, 48, cells, weights, st, outs=[vmem, hbm], more=more)
+
+
+def scatter_call(block, a, b, damp, cells, arrived, kept):
+    count = PIECES - RANGES
+    first = lax.broadcasted_iota(jnp.int32, (count, 1), 0) < block * RANGES
+    offsets = (((jnp.where(first, cells[:count], cells[RANGES:]) >> 7) + PAD) * 8).T
+    wide = (count * 8, 2 * NK)
     return run(
         scatter_kernel,
-        [smem, vmem, vmem, hbm],
-        (RANGES * V * SLAB, NK),
+        [smem, smem, smem, smem, vmem, vmem, hbm],
+        [(RANGES * V * SLAB, NK), (56, NK)],
         [((DEPTH, NK), f32), (wide, jnp.bfloat16), (wide, f32), (wide, f32)],
         48,
-        offsets_of(cells).T,
-        cells,
-        arrived.reshape(PIECES * 8, NK),
-        kept,
-        sems=1,
-    )
-
-
-def slab_call(a, b, damp, inverse, lines):
-    wide = ((NJ, CHUNK * NK), jnp.bfloat16)
-    return run(
-        slab_kernel,
-        [smem, smem, smem, vmem, vmem],
-        (RANGES * V * CJ * CHUNK, NK),
-        [((V, NJ * CHUNK, NK), f32), wide, wide],
-        20,
+        offsets,
         a,
         b,
         damp,
-        inverse,
-        lines,
+        cells,
+        arrived,
+        kept,
+        more=[pltpu.SemaphoreType.DMA],
     )
+
+
+def slab_call(factors, inverse, lines):
+    wide = ((NJ, CHUNK * NK), jnp.bfloat16)
+    scratch = [((V, NJ * CHUNK, NK), f32), wide, wide]
+    return run(slab_kernel, [vmem] * 3, (RANGES * V * CJ * CHUNK, NK), scratch, 20, factors, inverse, lines)
 
 
 def final_call(inverse, send, back):
     back = back.reshape(RANGES, V, CJ, CHUNK, NK)
-    return run(final_kernel, [vmem] * 3, (V * ROWS, NK), [], 20, inverse, send, back)
+    scratch = [((RANGES * V * SLAB, NK), f32), ((V * ROWS, NK), f32)]
+    more = [pltpu.SemaphoreType.DMA((V + 1,))]
+    return run(final_kernel, [vmem, hbm, vmem], [(V * ROWS, NK)], scratch, 48, inverse, send, back, outs=[hbm], more=more)[0]
 
 
 def exchange(x, axes):
@@ -312,9 +360,10 @@
     st = state.reshape(V * ROWS, NK)
     donated, kept = gather_call(donor_cell[0], donor_weight[0], st)
     arrived = exchange(donated, ("blk", "line"))
-    send = scatter_call(receptor_cell[0], arrived, kept)
+    block = lax.axis_index("blk")
+    send, factors = scatter_call(block, first_flux, second_flux, viscosity, receptor_cell[0], arrived, kept)
     lines = exchange(send, "line")
-    back = exchange(slab_call(first_flux, second_flux, viscosity, second_inverse[0], lines), "line")
+    back = exchange(slab_call(factors, second_inverse[0], lines), "line")
     return final_call(first_inverse[0], send, back).reshape(1, V, NI, CJ, NK)
 
 

time: 179 us -> 156 us (0.87)
  waiting for transfers between devices: 58.3 us -> 10.6 us
  blocking collectives: 37.9 us -> 77.2 us
  Pallas kernels: 62.6 us -> 52.5 us
  starting transfers between devices: 15 us -> 11.1 us
    all_to_all x2 -> x1, waiting for transfers between devices: 58.3 us -> 10.6 us  [exchange(): return lax.all_to_all(x, axes, split_axis=0, concat_axis=0, tiled=True)]
    all_to_all x1 -> x2, blocking collectives: 37.9 us -> 77.2 us  [exchange(): return lax.all_to_all(x, axes, split_axis=0, concat_axis=0, tiled=True)]
    pallas_call x4, Pallas kernels: 62.6 us -> 52.5 us  [run(): pl.pallas_call(kernel, out_shape=[jax.ShapeDtypeStruct(s, f32) for s in s...]
    all_to_all x2 -> x1, starting transfers between devices: 15 us -> 11.1 us  [exchange(): return lax.all_to_all(x, axes, split_axis=0, concat_axis=0, tiled=True)]
    unnamed x18 -> x20, local copies, waits for them, and re-layouts: 3.45 us -> 3.65 us
  transfers between devices with their start and end apart: 2 -> 1, of which waited for: 2 -> 1; matrix products, arithmetic and copies ran while one was open for 0% -> 0% of each run, Pallas kernels for 0% -> 0%
where the time goes in v5:
time: 156 us
  blocking collectives  77.2 us (49%)
  Pallas kernels  52.5 us (34%)
  starting transfers between devices  11.1 us (7%)
  waiting for transfers between devices  10.6 us (7%)
  local copies, waits for them, and re-layouts  3.66 us (2%)
    all_to_all x2, blocking collectives, exchange(): return lax.all_to_all(x, axes, split_axis=0, concat_axis=0, tiled=True)  77.2 us
    pallas_call x4, Pallas kernels, run(): pl.pallas_call(kernel, out_shape=[jax.ShapeDtypeStruct(s, f32) for s in s...  52.5 us
    all_to_all x1, starting transfers between devices, exchange(): return lax.all_to_all(x, axes, split_axis=0, concat_axis=0, tiled=True)  11.1 us
    all_to_all x1, waiting for transfers between devices, exchange(): return lax.all_to_all(x, axes, split_axis=0, concat_axis=0, tiled=True)  10.6 us
    unnamed x20, local copies, waits for them, and re-layouts  3.65 us
  transfers between devices with their start and end apart: 1, of which 1 were waited for; matrix products, arithmetic and copies ran while one was open for 0% of the time, Pallas kernels for 0%

profile of v5, /device:TPU:0, one launch (start us, length us, event | category | flops | bytes accessed | tf_op | source)
XLA Modules:
  0.0 156.0 jit_solution(6318790007783822161)
XLA Ops:
  0.0 0.0 copy-start.6
  0.0 0.0 copy-start.7
  0.0 0.0 copy-start
  0.0 1.8 %copy-done = f32[1,5,256,4,128]{4,3,2,1,0:T(4,128)S(1)} copy-done((f32[1,5,256,4,128]{4,3,2,1,0:T(4,128)S(1)}, f32[1,5,256,4,128]{4,3,2,1,0:T(4,128)}, u32[]{:S(2)}) %copy-start) | copy-done | bytes 2621464
  1.8 0.0 copy-start.3
  1.8 0.8 copy-done.3
  2.6 0.0 copy-start.4
  2.6 0.8 copy-done.4
  3.5 0.0 copy-start.1
  3.5 21.1 %shard_map.91 = (f32[128,1,640]{2,1,0:T(1,128)}, f32[8256,128]{1,0:T(8,128)}) custom-call(s32[128,128]{1,0:T(8,128)S(1)} %bitcast.32, f32[128,128]{1,0:T(8,128)S(1)} %bitcast.33, f32[5120,128]{1,0:T(8,128)S(1)} %bitcast.29), custom_call_target="tpu_custom_call" | custom-call | tf_op jit(solution)/shard_map/pallas_call | solution.py:288
  24.6 11.1 %all-to-all-start = ((f32[128,1,640]{2,1,0:T(1,128)}), f32[128,1,640]{2,1,0:T(1,128)S(1)}, u32[]{:S(2)}, u32[]{:S(2)}) async-start(f32[128,1,640]{2,1,0:T(1,128)} %get-tuple-element.9), calls=%async_computation | async-start | bytes 655360 | tf_op jit(solution)/shard_map/all_to_all | solution.py:346
  36.4 0.0 copy-done.6
  36.4 0.0 copy-done.7
  36.5 0.0 copy-done.1
  36.5 0.1 copy.14
  36.6 0.1 copy.15
  36.7 10.6 %all-to-all-done.arrived_ref = f32[128,1,640]{2,1,0:T(1,128)S(1)} async-done(((f32[128,1,640]{2,1,0:T(1,128)}), f32[128,1,640]{2,1,0:T(1,128)S(1)}, u32[]{:S(2)}, u32[]{:S(2)}) %all-to-all-start) | async-done | bytes 327712 | tf_op jit(solution)/shard_map/all_to_all | solution.py:346
  47.3 22.1 %shard_map.92 = (f32[5760,128]{1,0:T(8,128)S(1)}, f32[56,128]{1,0:T(8,128)S(1)}) custom-call(s32[128,112]{1,0:T(8,128)S(1)} %fusion.3.offset_ref, f32[1,5,5]{2,1,0:T(8,128)S(1)} %copy.12.a_ref, f32[1,5,5]{2,1,0:T(8,128)S(1)} %copy.13.b_ref, f32[1]{0:T(128)S(6)} %copy.16.damp_ref, s32[128,128]{1,0:T(8,128)S(1)} %bitcast.30, ...), custom_call_target="tpu_custom_call" | custom-call | tf_op jit(solution)/shard_map/pallas_call | solution.py:288
  69.5 0.0 copy-start.5
  69.5 40.6 %all_to_all.25 = f32[16,360,128]{2,1,0:T(8,128)S(1)} all-to-all(f32[16,360,128]{2,1,0:T(8,128)S(1)} %bitcast.26), channel_id=1, replica_groups=mesh['blk'=8,'line'=16] {'line'}, dimensions={0} | all-to-all | bytes 5898240 | tf_op jit(solution)/shard_map/all_to_all | solution.py:346
  110.0 0.0 copy-done.5
  110.0 6.7 %shard_map.93 = f32[5120,128]{1,0:T(8,128)S(1)} custom-call(f32[56,128]{1,0:T(8,128)S(1)} %get-tuple-element.12.factor_ref, f32[64,64]{1,0:T(8,128)S(1)} %bitcast.34, f32[5760,128]{1,0:T(8,128)S(1)} %bitcast.25), custom_call_target="tpu_custom_call" | custom-call | tf_op jit(solution)/shard_map/pallas_call | solution.py:288
  116.7 0.0 copy-start.2
  116.7 36.7 %all_to_all.26 = f32[16,320,128]{2,1,0:T(8,128)S(1)} all-to-all(f32[16,320,128]{2,1,0:T(8,128)S(1)} %bitcast.27), channel_id=1, replica_groups=mesh['blk'=8,'line'=16] {'line'}, dimensions={0} | all-to-all | bytes 5242880 | tf_op jit(solution)/shard_map/all_to_all | solution.py:346
  153.4 0.0 copy-done.2
  153.4 2.6 %shard_map.94 = f32[5120,128]{1,0:T(8,128)} custom-call(f32[256,256]{1,0:T(8,128)S(1)} %bitcast.31, f32[5760,128]{1,0:T(8,128)S(1)} %get-tuple-element.11.send_hbm, f32[16,5,4,16,128]{4,3,2,1,0:T(8,128)S(1)} %bitcast.28), custom_call_target="tpu_custom_call" | custom-call | tf_op jit(solution)/shard_map/pallas_call | solution.py:288
  (5 shorter events, 0.0 us)
Async XLA Ops:
  0.0 36.4 %copy-start.6 = (f32[1,5,5]{2,0,1:T(1,128)S(1)}, f32[1,5,5]{2,0,1:T(1,128)}, u32[]{:S(2)}) copy-start(f32[1,5,5]{2,0,1:T(1,128)} %param.10) | copy-start | bytes 304
  0.0 36.4 %copy-start.7 = (f32[1,5,5]{2,0,1:T(1,128)S(1)}, f32[1,5,5]{2,0,1:T(1,128)}, u32[]{:S(2)}) copy-start(f32[1,5,5]{2,0,1:T(1,128)} %param.11) | copy-start | bytes 304
  0.0 1.8 %copy-start = (f32[1,5,256,4,128]{4,3,2,1,0:T(4,128)S(1)}, f32[1,5,256,4,128]{4,3,2,1,0:T(4,128)}, u32[]{:S(2)}) copy-start(f32[1,5,256,4,128]{4,3,2,1,0:T(4,128)} %param.9) | copy-start | bytes 7864324
  1.8 0.8 copy-start.3
  2.6 0.8 copy-start.4
  3.5 33.0 %copy-start.1 = (s32[1,128,128]{2,1,0:T(8,128)S(1)}, s32[1,128,128]{2,1,0:T(8,128)}, u32[]{:S(2)}) copy-start(s32[1,128,128]{2,1,0:T(8,128)} %param.17) | copy-start | bytes 196612
  24.6 22.7 %all-to-all-start = ((f32[128,1,640]{2,1,0:T(1,128)}), f32[128,1,640]{2,1,0:T(1,128)S(1)}, u32[]{:S(2)}, u32[]{:S(2)}) async-start(f32[128,1,640]{2,1,0:T(1,128)} %get-tuple-element.9), calls=%async_computation | async-start | bytes 655360 | tf_op jit(solution)/shard_map/all_to_all | solution.py:346
  69.5 40.6 %copy-start.5 = (f32[1,64,64]{2,1,0:T(8,128)S(1)}, f32[1,64,64]{2,1,0:T(8,128)}, u32[]{:S(2)}) copy-start(f32[1,64,64]{2,1,0:T(8,128)} %param.14) | copy-start | bytes 49156
  116.7 36.7 %copy-start.2 = (f32[1,256,256]{2,1,0:T(8,128)S(1)}, f32[1,256,256]{2,1,0:T(8,128)}, u32[]{:S(2)}) copy-start(f32[1,256,256]{2,1,0:T(8,128)} %param.13) | copy-start | bytes 786436

commit v6 on v5

--- a/solution.py
+++ b/solution.py
@@ -23,8 +23,10 @@
     copies = [
         pltpu.make_async_copy(cell_hbm, lane_ref, sems.at[0]),
         pltpu.make_async_copy(weight_hbm, weight_ref, sems.at[1]),
-        pltpu.make_async_copy(st_hbm, st_ref, sems.at[2]),
     ]
+    for v in range(V):
+        rows = pl.ds(v * ROWS, ROWS)
+        copies.append(pltpu.make_async_copy(st_hbm.at[rows, :], st_ref.at[rows, :], sems.at[2 + v]))
     for copy in copies:
         copy.start()
     block = lax.axis_index("blk")
@@ -52,21 +54,21 @@
 
     lax.fori_loop(0, PIECES // 32, before, 0)
 
-    copies[2].wait()
     for t in range(PAD):
         tiles[t * 8 : t * 8 + 8, :] = jnp.zeros((8, 128), f32)
         tiles[DEPTH - t * 8 - 8 : DEPTH - t * 8, :] = jnp.zeros((8, 128), f32)
-
-    def lay(b, carry):
-        for t in range(2):
-            c = b * 2 + t
-            for v in range(V):
+    for v in range(V):
+        copies[2 + v].wait()
+
+        def lay(b, carry):
+            for t in range(8):
+                c = b * 8 + t
                 tiles[pl.ds(PAD * 8 + c * 64 + v, 8, stride=8), :] = st_ref[
                     pl.ds(pl.multiple_of(v * ROWS + c * 8, 8), 8), :
                 ]
-        return carry
-
-    lax.fori_loop(0, ROWS // 16, lay, 0)
+            return carry
+
+        lax.fori_loop(0, ROWS // 64, lay, 0)
     keep = pltpu.make_async_copy(tiles, kept_ref, sems.at[2])
     keep.start()
     offsets.wait()
@@ -89,7 +91,7 @@
             picked[m, h] = acc * jnp.broadcast_to(mix[h, pl.ds(m, 1), :], (8, 128))
         return carry
 
-    lax.fori_loop(0, PIECES - RANGES, piece, 0, unroll=8)
+    lax.fori_loop(0, PIECES - RANGES, piece, 0, unroll=16)
 
     def after(b, carry):
         for t in range(16):
@@ -302,9 +304,9 @@
 def gather_call(cells, weights, st):
     scratch = [LANES, ((PIECES, SLOTS), f32), ((V * ROWS, NK), f32), LANES, ((DEPTH, NK), f32)]
     scratch += [((2, PIECES, NK), jnp.int32), ((2, PIECES, NK), f32), ((PIECES, 2, 8, NK), f32)]
-    more = [pltpu.SMEM((PIECES, SLOTS), jnp.int32), pltpu.SemaphoreType.DMA((3,))]
+    more = [pltpu.SMEM((PIECES, SLOTS), jnp.int32), pltpu.SemaphoreType.DMA((2 + V,))]
     shapes = [(PIECES, 1, V * SLOTS), (DEPTH, NK)]
-    return run(gather_kernel, [hbm] * 3, shapes, scratch, 48, cells, weights, st, outs=[vmem, hbm], more=more)
+    return run(gather_kernel, [hbm] * 3, shapes, scratch, 60, cells, weights, st, outs=[vmem, hbm], more=more)
 
 
 def scatter_call(block, a, b, damp, cells, arrived, kept):

time: 156 us -> 153 us (0.981)
  local copies, waits for them, and re-layouts: 3.66 us -> 0.22 us
    unnamed x20 -> x14, local copies, waits for them, and re-layouts: 3.65 us -> 0.21 us
where the time goes in v6:
time: 153 us
  blocking collectives  77.2 us (50%)
  Pallas kernels  52.6 us (34%)
  starting transfers between devices  11.1 us (7%)
  waiting for transfers between devices  10.6 us (7%)
    all_to_all x2, blocking collectives, exchange(): return lax.all_to_all(x, axes, split_axis=0, concat_axis=0, tiled=True)  77.2 us
    pallas_call x4, Pallas kernels, run(): pl.pallas_call(kernel, out_shape=[jax.ShapeDtypeStruct(s, f32) for s in s...  52.6 us
    all_to_all x1, starting transfers between devices, exchange(): return lax.all_to_all(x, axes, split_axis=0, concat_axis=0, tiled=True)  11.1 us
    all_to_all x1, waiting for transfers between devices, exchange(): return lax.all_to_all(x, axes, split_axis=0, concat_axis=0, tiled=True)  10.6 us
  transfers between devices with their start and end apart: 1, of which 1 were waited for; matrix products, arithmetic and copies ran while one was open for 0% of the time, Pallas kernels for 0%

profile of v6, /device:TPU:0, one launch (start us, length us, event | category | flops | bytes accessed | tf_op | source)
XLA Modules:
  0.0 152.6 jit_solution(18198059087040428066)
XLA Ops:
  0.0 0.0 copy-start.3
  0.0 0.0 copy-start.4
  0.0 0.0 copy-start
  0.0 21.2 %shard_map.91 = (f32[128,1,640]{2,1,0:T(1,128)}, f32[8256,128]{1,0:T(8,128)}) custom-call(s32[128,128]{1,0:T(8,128)} %bitcast.33, f32[128,128]{1,0:T(8,128)} %bitcast.34, f32[5120,128]{1,0:T(8,128)} %bitcast.32), custom_call_target="tpu_custom_call" | custom-call | tf_op jit(solution)/shard_map/pallas_call | solution.py:290
  21.2 11.1 %all-to-all-start = ((f32[128,1,640]{2,1,0:T(1,128)}), f32[128,1,640]{2,1,0:T(1,128)S(1)}, u32[]{:S(2)}, u32[]{:S(2)}) async-start(f32[128,1,640]{2,1,0:T(1,128)} %get-tuple-element.9), calls=%async_computation | async-start | bytes 655360 | tf_op jit(solution)/shard_map/all_to_all | solution.py:348
  33.0 0.0 copy-done.3
  33.0 0.0 copy-done.4
  33.0 0.0 copy-done
  33.1 0.1 copy.14
  33.2 0.1 copy.15
  33.3 10.6 %all-to-all-done.arrived_ref = f32[128,1,640]{2,1,0:T(1,128)S(1)} async-done(((f32[128,1,640]{2,1,0:T(1,128)}), f32[128,1,640]{2,1,0:T(1,128)S(1)}, u32[]{:S(2)}, u32[]{:S(2)}) %all-to-all-start) | async-done | bytes 327712 | tf_op jit(solution)/shard_map/all_to_all | solution.py:348
  43.9 22.1 %shard_map.92 = (f32[5760,128]{1,0:T(8,128)S(1)}, f32[56,128]{1,0:T(8,128)S(1)}) custom-call(s32[128,112]{1,0:T(8,128)S(1)} %fusion.3.offset_ref, f32[1,5,5]{2,1,0:T(8,128)S(1)} %copy.12.a_ref, f32[1,5,5]{2,1,0:T(8,128)S(1)} %copy.13.b_ref, f32[1]{0:T(128)S(6)} %copy.16.damp_ref, s32[128,128]{1,0:T(8,128)S(1)} %bitcast.29, ...), custom_call_target="tpu_custom_call" | custom-call | tf_op jit(solution)/shard_map/pallas_call | solution.py:290
  66.1 0.0 copy-start.2
  66.1 40.5 %all_to_all.25 = f32[16,360,128]{2,1,0:T(8,128)S(1)} all-to-all(f32[16,360,128]{2,1,0:T(8,128)S(1)} %bitcast.26), channel_id=1, replica_groups=mesh['blk'=8,'line'=16] {'line'}, dimensions={0} | all-to-all | bytes 5898240 | tf_op jit(solution)/shard_map/all_to_all | solution.py:348
  106.6 0.0 copy-done.2
  106.6 6.7 %shard_map.93 = f32[5120,128]{1,0:T(8,128)S(1)} custom-call(f32[56,128]{1,0:T(8,128)S(1)} %get-tuple-element.12.factor_ref, f32[64,64]{1,0:T(8,128)S(1)} %bitcast.31, f32[5760,128]{1,0:T(8,128)S(1)} %bitcast.25), custom_call_target="tpu_custom_call" | custom-call | tf_op jit(solution)/shard_map/pallas_call | solution.py:290
  113.3 0.0 copy-start.1
  113.3 36.7 %all_to_all.26 = f32[16,320,128]{2,1,0:T(8,128)S(1)} all-to-all(f32[16,320,128]{2,1,0:T(8,128)S(1)} %bitcast.27), channel_id=1, replica_groups=mesh['blk'=8,'line'=16] {'line'}, dimensions={0} | all-to-all | bytes 5242880 | tf_op jit(solution)/shard_map/all_to_all | solution.py:348
  150.0 0.0 copy-done.1
  150.0 2.6 %shard_map.94 = f32[5120,128]{1,0:T(8,128)} custom-call(f32[256,256]{1,0:T(8,128)S(1)} %bitcast.30, f32[5760,128]{1,0:T(8,128)S(1)} %get-tuple-element.11.send_hbm, f32[16,5,4,16,128]{4,3,2,1,0:T(8,128)S(1)} %bitcast.28), custom_call_target="tpu_custom_call" | custom-call | tf_op jit(solution)/shard_map/pallas_call | solution.py:290
  (5 shorter events, 0.0 us)
Async XLA Ops:
  0.0 33.0 %copy-start.3 = (f32[1,5,5]{2,0,1:T(1,128)S(1)}, f32[1,5,5]{2,0,1:T(1,128)}, u32[]{:S(2)}) copy-start(f32[1,5,5]{2,0,1:T(1,128)} %param.10) | copy-start | bytes 304
  0.0 33.0 %copy-start.4 = (f32[1,5,5]{2,0,1:T(1,128)S(1)}, f32[1,5,5]{2,0,1:T(1,128)}, u32[]{:S(2)}) copy-start(f32[1,5,5]{2,0,1:T(1,128)} %param.11) | copy-start | bytes 304
  0.0 33.0 %copy-start = (s32[1,128,128]{2,1,0:T(8,128)S(1)}, s32[1,128,128]{2,1,0:T(8,128)}, u32[]{:S(2)}) copy-start(s32[1,128,128]{2,1,0:T(8,128)} %param.17) | copy-start | bytes 196612
  21.2 22.7 %all-to-all-start = ((f32[128,1,640]{2,1,0:T(1,128)}), f32[128,1,640]{2,1,0:T(1,128)S(1)}, u32[]{:S(2)}, u32[]{:S(2)}) async-start(f32[128,1,640]{2,1,0:T(1,128)} %get-tuple-element.9), calls=%async_computation | async-start | bytes 655360 | tf_op jit(solution)/shard_map/all_to_all | solution.py:348
  66.1 40.6 %copy-start.2 = (f32[1,64,64]{2,1,0:T(8,128)S(1)}, f32[1,64,64]{2,1,0:T(8,128)}, u32[]{:S(2)}) copy-start(f32[1,64,64]{2,1,0:T(8,128)} %param.14) | copy-start | bytes 49156
  113.3 36.7 %copy-start.1 = (f32[1,256,256]{2,1,0:T(8,128)S(1)}, f32[1,256,256]{2,1,0:T(8,128)}, u32[]{:S(2)}) copy-start(f32[1,256,256]{2,1,0:T(8,128)} %param.13) | copy-start | bytes 786436

commit v7 on v6

--- a/solution.py
+++ b/solution.py
@@ -91,7 +91,7 @@
             picked[m, h] = acc * jnp.broadcast_to(mix[h, pl.ds(m, 1), :], (8, 128))
         return carry
 
-    lax.fori_loop(0, PIECES - RANGES, piece, 0, unroll=16)
+    lax.fori_loop(0, PIECES - RANGES, piece, 0, unroll=28)
 
     def after(b, carry):
         for t in range(16):
@@ -109,7 +109,9 @@
     keep.wait()
 
 
-def scatter_kernel(offset_ref, a_ref, b_ref, damp_ref, cell_ref, arrived_ref, kept_ref, send_ref, factor_ref, tiles, parts, ping, pong, sem):
+def scatter_kernel(offset_vmem, a_ref, b_ref, damp_ref, cell_ref, arrived_ref, kept_ref, send_ref, factor_ref, tiles, parts, ping, pong, offset_ref, sem, offset_sem):
+    offsets = pltpu.make_async_copy(offset_vmem, offset_ref, offset_sem)
+    offsets.start()
     block = lax.axis_index("blk")
     keep = pltpu.make_async_copy(kept_ref, tiles, sem)
     keep.start()
@@ -169,6 +171,7 @@
     first = ones(0)
     for g in range(4):
         spread(first, ping, g)
+    offsets.wait()
     keep.wait()
 
     def both(i, carry):
@@ -203,7 +206,7 @@
     return dot(x[0], y[0]) + (dot(x[0], y[1]) + dot(x[1], y[0]))
 
 
-def slab_kernel(factor_ref, inverse_ref, in_ref, out_ref, rhs, coarse, fine):
+def slab_kernel(factor_ref, inverse_ref, in_ref, out_ref, rhs, wide):
     lane = lax.broadcasted_iota(jnp.int32, (CHUNK, 128), 1)
 
     def factor(r):
@@ -239,14 +242,18 @@
                 rhs[u, pl.ds(pl.multiple_of((s * CJ + j) * CHUNK, CHUNK), CHUNK), :] = r
         return carry
 
-    lax.fori_loop(0, RANGES, one, 0)
+    lax.fori_loop(0, RANGES, one, 0, unroll=2)
     matrix = halves(jnp.concatenate([inverse_ref[pl.ds(j, RANGES, stride=CJ), :] for j in range(CJ)], axis=0))
+    matrix = jnp.concatenate([matrix[0], matrix[0], matrix[1]], axis=1)
     step = V * CJ * CHUNK
     for u in range(V):
         for i in range(CHUNK):
             columns = slice(i * NK, (i + 1) * NK)
-            coarse[:, columns], fine[:, columns] = halves(rhs[u, pl.ds(i, NJ, stride=CHUNK), :])
-        solved = product(matrix, (coarse[...], fine[...]))
+            coarse, fine = halves(rhs[u, pl.ds(i, NJ, stride=CHUNK), :])
+            wide[0:NJ, columns] = coarse
+            wide[NJ : 2 * NJ, columns] = fine
+            wide[2 * NJ : 3 * NJ, columns] = coarse
+        solved = jnp.dot(matrix, wide[...], preferred_element_type=f32)
         for j in range(CJ):
             for i in range(CHUNK):
                 for s in range(0, RANGES, 8):
@@ -311,12 +318,13 @@
 
 def scatter_call(block, a, b, damp, cells, arrived, kept):
     count = PIECES - RANGES
-    first = lax.broadcasted_iota(jnp.int32, (count, 1), 0) < block * RANGES
-    offsets = (((jnp.where(first, cells[:count], cells[RANGES:]) >> 7) + PAD) * 8).T
+    first = lax.broadcasted_iota(jnp.int32, (PIECES, 1), 0) < block * RANGES
+    shifted = jnp.concatenate([cells[RANGES:], cells[:RANGES]])
+    offsets = (((jnp.where(first, cells, shifted) >> 7) + PAD) * 8).T
     wide = (count * 8, 2 * NK)
     return run(
         scatter_kernel,
-        [smem, smem, smem, smem, vmem, vmem, hbm],
+        [vmem, smem, smem, smem, vmem, vmem, hbm],
         [(RANGES * V * SLAB, NK), (56, NK)],
         [((DEPTH, NK), f32), (wide, jnp.bfloat16), (wide, f32), (wide, f32)],
         48,
@@ -327,13 +335,12 @@
         cells,
         arrived,
         kept,
-        more=[pltpu.SemaphoreType.DMA],
+        more=[pltpu.SMEM((SLOTS, PIECES), jnp.int32), pltpu.SemaphoreType.DMA, pltpu.SemaphoreType.DMA],
     )
 
 
 def slab_call(factors, inverse, lines):
-    wide = ((NJ, CHUNK * NK), jnp.bfloat16)
-    scratch = [((V, NJ * CHUNK, NK), f32), wide, wide]
+    scratch = [((V, NJ * CHUNK, NK), f32), ((3 * NJ, CHUNK * NK), jnp.bfloat16)]
     return run(slab_kernel, [vmem] * 3, (RANGES * V * CJ * CHUNK, NK), scratch, 20, factors, inverse, lines)
 
 

time: 153 us -> 151 us (0.987)
  Pallas kernels: 52.6 us -> 50.7 us
    pallas_call x4, Pallas kernels: 52.6 us -> 50.7 us  [run(): pl.pallas_call(kernel, out_shape=[jax.ShapeDtypeStruct(s, f32) for s in s...]
where the time goes in v7:
time: 151 us
  blocking collectives  77.3 us (51%)
  Pallas kernels  50.7 us (34%)
  starting transfers between devices  11.2 us (7%)
  waiting for transfers between devices  10.6 us (7%)
    all_to_all x2, blocking collectives, exchange(): return lax.all_to_all(x, axes, split_axis=0, concat_axis=0, tiled=True)  77.3 us
    pallas_call x4, Pallas kernels, run(): pl.pallas_call(kernel, out_shape=[jax.ShapeDtypeStruct(s, f32) for s in s...  50.7 us
    all_to_all x1, starting transfers between devices, exchange(): return lax.all_to_all(x, axes, split_axis=0, concat_axis=0, tiled=True)  11.2 us
    all_to_all x1, waiting for transfers between devices, exchange(): return lax.all_to_all(x, axes, split_axis=0, concat_axis=0, tiled=True)  10.6 us
  transfers between devices with their start and end apart: 1, of which 1 were waited for; matrix products, arithmetic and copies ran while one was open for 0% of the time, Pallas kernels for 0%

profile of v7, /device:TPU:0, one launch (start us, length us, event | category | flops | bytes accessed | tf_op | source)
XLA Modules:
  0.0 150.7 jit_solution(1333618069079748715)
XLA Ops:
  0.0 0.0 copy-start
  0.0 0.0 copy-start.3
  0.0 0.0 copy-start.4
  0.0 21.0 %shard_map.91 = (f32[128,1,640]{2,1,0:T(1,128)}, f32[8256,128]{1,0:T(8,128)}) custom-call(s32[128,128]{1,0:T(8,128)} %bitcast.26, f32[128,128]{1,0:T(8,128)} %bitcast.27, f32[5120,128]{1,0:T(8,128)} %bitcast.25), custom_call_target="tpu_custom_call" | custom-call | tf_op jit(solution)/shard_map/pallas_call | solution.py:297
  21.0 11.2 %all-to-all-start = ((f32[128,1,640]{2,1,0:T(1,128)}), f32[128,1,640]{2,1,0:T(1,128)S(1)}, u32[]{:S(2)}, u32[]{:S(2)}) async-start(f32[128,1,640]{2,1,0:T(1,128)} %get-tuple-element.9), calls=%async_computation | async-start | bytes 655360 | tf_op jit(solution)/shard_map/all_to_all | solution.py:355
  32.1 0.0 copy-done
  32.8 0.0 copy-done.3
  32.8 0.0 copy-done.4
  32.9 0.1 fusion.3
  33.0 0.1 copy.10.offset_vmem
  33.1 10.6 %all-to-all-done.arrived_ref = f32[128,1,640]{2,1,0:T(1,128)S(1)} async-done(((f32[128,1,640]{2,1,0:T(1,128)}), f32[128,1,640]{2,1,0:T(1,128)S(1)}, u32[]{:S(2)}, u32[]{:S(2)}) %all-to-all-start) | async-done | bytes 327712 | tf_op jit(solution)/shard_map/all_to_all | solution.py:355
  43.7 21.1 %shard_map.92 = (f32[5760,128]{1,0:T(8,128)S(1)}, f32[56,128]{1,0:T(8,128)S(1)}) custom-call(s32[128,128]{1,0:T(8,128)S(1)} %copy.10.offset_vmem, f32[1,5,5]{2,1,0:T(8,128)S(1)} %copy.11.a_ref, f32[1,5,5]{2,1,0:T(8,128)S(1)} %copy.12.b_ref, f32[1]{0:T(128)S(6)} %copy.13.damp_ref, s32[128,128]{1,0:T(8,128)S(1)} %bitcast.22, ...), custom_call_target="tpu_custom_call" | custom-call | tf_op jit(solution)/shard_map/pallas_call | solution.py:297
  64.8 0.0 copy-start.2
  64.8 40.6 %all_to_all.25 = f32[16,360,128]{2,1,0:T(8,128)S(1)} all-to-all(f32[16,360,128]{2,1,0:T(8,128)S(1)} %bitcast.19), channel_id=1, replica_groups=mesh['blk'=8,'line'=16] {'line'}, dimensions={0} | all-to-all | bytes 5898240 | tf_op jit(solution)/shard_map/all_to_all | solution.py:355
  105.4 0.0 copy-done.2
  105.4 6.1 %shard_map.93 = f32[5120,128]{1,0:T(8,128)S(1)} custom-call(f32[56,128]{1,0:T(8,128)S(1)} %get-tuple-element.12.factor_ref, f32[64,64]{1,0:T(8,128)S(1)} %bitcast.24, f32[5760,128]{1,0:T(8,128)S(1)} %bitcast.18), custom_call_target="tpu_custom_call" | custom-call | tf_op jit(solution)/shard_map/pallas_call | solution.py:297
  111.4 0.0 copy-start.1
  111.4 36.7 %all_to_all.26 = f32[16,320,128]{2,1,0:T(8,128)S(1)} all-to-all(f32[16,320,128]{2,1,0:T(8,128)S(1)} %bitcast.20), channel_id=1, replica_groups=mesh['blk'=8,'line'=16] {'line'}, dimensions={0} | all-to-all | bytes 5242880 | tf_op jit(solution)/shard_map/all_to_all | solution.py:355
  148.1 0.0 copy-done.1
  148.1 2.6 %shard_map.94 = f32[5120,128]{1,0:T(8,128)} custom-call(f32[256,256]{1,0:T(8,128)S(1)} %bitcast.23, f32[5760,128]{1,0:T(8,128)S(1)} %get-tuple-element.11.send_hbm, f32[16,5,4,16,128]{4,3,2,1,0:T(8,128)S(1)} %bitcast.21), custom_call_target="tpu_custom_call" | custom-call | tf_op jit(solution)/shard_map/pallas_call | solution.py:297
  (5 shorter events, 0.0 us)
Async XLA Ops:
  0.0 32.1 %copy-start = (s32[1,128,128]{2,1,0:T(8,128)S(1)}, s32[1,128,128]{2,1,0:T(8,128)}, u32[]{:S(2)}) copy-start(s32[1,128,128]{2,1,0:T(8,128)} %param.17) | copy-start | bytes 196612
  0.0 32.8 %copy-start.3 = (f32[1,5,5]{2,0,1:T(1,128)S(1)}, f32[1,5,5]{2,0,1:T(1,128)}, u32[]{:S(2)}) copy-start(f32[1,5,5]{2,0,1:T(1,128)} %param.10) | copy-start | bytes 304
  0.0 32.8 %copy-start.4 = (f32[1,5,5]{2,0,1:T(1,128)S(1)}, f32[1,5,5]{2,0,1:T(1,128)}, u32[]{:S(2)}) copy-start(f32[1,5,5]{2,0,1:T(1,128)} %param.11) | copy-start | bytes 304
  21.0 22.7 %all-to-all-start = ((f32[128,1,640]{2,1,0:T(1,128)}), f32[128,1,640]{2,1,0:T(1,128)S(1)}, u32[]{:S(2)}, u32[]{:S(2)}) async-start(f32[128,1,640]{2,1,0:T(1,128)} %get-tuple-element.9), calls=%async_computation | async-start | bytes 655360 | tf_op jit(solution)/shard_map/all_to_all | solution.py:355
  64.8 40.6 %copy-start.2 = (f32[1,64,64]{2,1,0:T(8,128)S(1)}, f32[1,64,64]{2,1,0:T(8,128)}, u32[]{:S(2)}) copy-start(f32[1,64,64]{2,1,0:T(8,128)} %param.14) | copy-start | bytes 49156
  111.4 36.7 %copy-start.1 = (f32[1,256,256]{2,1,0:T(8,128)S(1)}, f32[1,256,256]{2,1,0:T(8,128)}, u32[]{:S(2)}) copy-start(f32[1,256,256]{2,1,0:T(8,128)} %param.13) | copy-start | bytes 786436

commit v8 on v7

--- a/solution.py
+++ b/solution.py
@@ -191,7 +191,7 @@
                 ]
         return carry
 
-    lax.fori_loop(0, RANGES, slab, 0)
+    lax.fori_loop(0, RANGES, slab, 0, unroll=2)
 
 
 def halves(x):
@@ -242,7 +242,7 @@
                 rhs[u, pl.ds(pl.multiple_of((s * CJ + j) * CHUNK, CHUNK), CHUNK), :] = r
         return carry
 
-    lax.fori_loop(0, RANGES, one, 0, unroll=2)
+    lax.fori_loop(0, RANGES, one, 0, unroll=4)
     matrix = halves(jnp.concatenate([inverse_ref[pl.ds(j, RANGES, stride=CJ), :] for j in range(CJ)], axis=0))
     matrix = jnp.concatenate([matrix[0], matrix[0], matrix[1]], axis=1)
     step = V * CJ * CHUNK

time: 151 us -> 151 us (level)
  no operation moved by 1% of the time
where the time goes in v8:
time: 151 us; the launch traced here: 150 us
  blocking collectives  77.3 us (51%)
  Pallas kernels  50.4 us (33%)
  starting transfers between devices  11.2 us (7%)
  waiting for transfers between devices  10.6 us (7%)
    all_to_all x2, blocking collectives, exchange(): return lax.all_to_all(x, axes, split_axis=0, concat_axis=0, tiled=True)  77.3 us
    pallas_call x4, Pallas kernels, run(): pl.pallas_call(kernel, out_shape=[jax.ShapeDtypeStruct(s, f32) for s in s...  50.4 us
    all_to_all x1, starting transfers between devices, exchange(): return lax.all_to_all(x, axes, split_axis=0, concat_axis=0, tiled=True)  11.2 us
    all_to_all x1, waiting for transfers between devices, exchange(): return lax.all_to_all(x, axes, split_axis=0, concat_axis=0, tiled=True)  10.6 us
  transfers between devices with their start and end apart: 1, of which 1 were waited for; matrix products, arithmetic and copies ran while one was open for 0% of the time, Pallas kernels for 0%

profile of v8, /device:TPU:0, one launch (start us, length us, event | category | flops | bytes accessed | tf_op | source)
XLA Modules:
  0.0 150.5 jit_solution(11274557887233108942)
XLA Ops:
  0.0 0.0 copy-start
  0.0 0.0 copy-start.3
  0.0 0.0 copy-start.4
  0.0 21.0 %shard_map.91 = (f32[128,1,640]{2,1,0:T(1,128)}, f32[8256,128]{1,0:T(8,128)}) custom-call(s32[128,128]{1,0:T(8,128)} %bitcast.26, f32[128,128]{1,0:T(8,128)} %bitcast.27, f32[5120,128]{1,0:T(8,128)} %bitcast.25), custom_call_target="tpu_custom_call" | custom-call | tf_op jit(solution)/shard_map/pallas_call | solution.py:297
  21.0 11.2 %all-to-all-start = ((f32[128,1,640]{2,1,0:T(1,128)}), f32[128,1,640]{2,1,0:T(1,128)S(1)}, u32[]{:S(2)}, u32[]{:S(2)}) async-start(f32[128,1,640]{2,1,0:T(1,128)} %get-tuple-element.9), calls=%async_computation | async-start | bytes 655360 | tf_op jit(solution)/shard_map/all_to_all | solution.py:355
  32.1 0.0 copy-done
  32.8 0.0 copy-done.3
  32.8 0.0 copy-done.4
  32.9 0.1 fusion.3
  33.0 0.1 copy.10.offset_vmem
  33.1 10.6 %all-to-all-done.arrived_ref = f32[128,1,640]{2,1,0:T(1,128)S(1)} async-done(((f32[128,1,640]{2,1,0:T(1,128)}), f32[128,1,640]{2,1,0:T(1,128)S(1)}, u32[]{:S(2)}, u32[]{:S(2)}) %all-to-all-start) | async-done | bytes 327712 | tf_op jit(solution)/shard_map/all_to_all | solution.py:355
  43.7 21.0 %shard_map.92 = (f32[5760,128]{1,0:T(8,128)S(1)}, f32[56,128]{1,0:T(8,128)S(1)}) custom-call(s32[128,128]{1,0:T(8,128)S(1)} %copy.10.offset_vmem, f32[1,5,5]{2,1,0:T(8,128)S(1)} %copy.11.a_ref, f32[1,5,5]{2,1,0:T(8,128)S(1)} %copy.12.b_ref, f32[1]{0:T(128)S(6)} %copy.13.damp_ref, s32[128,128]{1,0:T(8,128)S(1)} %bitcast.22, ...), custom_call_target="tpu_custom_call" | custom-call | tf_op jit(solution)/shard_map/pallas_call | solution.py:297
  64.7 0.0 copy-start.2
  64.7 40.6 %all_to_all.25 = f32[16,360,128]{2,1,0:T(8,128)S(1)} all-to-all(f32[16,360,128]{2,1,0:T(8,128)S(1)} %bitcast.19), channel_id=1, replica_groups=mesh['blk'=8,'line'=16] {'line'}, dimensions={0} | all-to-all | bytes 5898240 | tf_op jit(solution)/shard_map/all_to_all | solution.py:355
  105.3 0.0 copy-done.2
  105.3 5.9 %shard_map.93 = f32[5120,128]{1,0:T(8,128)S(1)} custom-call(f32[56,128]{1,0:T(8,128)S(1)} %get-tuple-element.12.factor_ref, f32[64,64]{1,0:T(8,128)S(1)} %bitcast.24, f32[5760,128]{1,0:T(8,128)S(1)} %bitcast.18), custom_call_target="tpu_custom_call" | custom-call | tf_op jit(solution)/shard_map/pallas_call | solution.py:297
  111.2 0.0 copy-start.1
  111.2 36.7 %all_to_all.26 = f32[16,320,128]{2,1,0:T(8,128)S(1)} all-to-all(f32[16,320,128]{2,1,0:T(8,128)S(1)} %bitcast.20), channel_id=1, replica_groups=mesh['blk'=8,'line'=16] {'line'}, dimensions={0} | all-to-all | bytes 5242880 | tf_op jit(solution)/shard_map/all_to_all | solution.py:355
  147.9 0.0 copy-done.1
  147.9 2.6 %shard_map.94 = f32[5120,128]{1,0:T(8,128)} custom-call(f32[256,256]{1,0:T(8,128)S(1)} %bitcast.23, f32[5760,128]{1,0:T(8,128)S(1)} %get-tuple-element.11.send_hbm, f32[16,5,4,16,128]{4,3,2,1,0:T(8,128)S(1)} %bitcast.21), custom_call_target="tpu_custom_call" | custom-call | tf_op jit(solution)/shard_map/pallas_call | solution.py:297
  (5 shorter events, 0.0 us)
Async XLA Ops:
  0.0 32.1 %copy-start = (s32[1,128,128]{2,1,0:T(8,128)S(1)}, s32[1,128,128]{2,1,0:T(8,128)}, u32[]{:S(2)}) copy-start(s32[1,128,128]{2,1,0:T(8,128)} %param.17) | copy-start | bytes 196612
  0.0 32.8 %copy-start.3 = (f32[1,5,5]{2,0,1:T(1,128)S(1)}, f32[1,5,5]{2,0,1:T(1,128)}, u32[]{:S(2)}) copy-start(f32[1,5,5]{2,0,1:T(1,128)} %param.10) | copy-start | bytes 304
  0.0 32.8 %copy-start.4 = (f32[1,5,5]{2,0,1:T(1,128)S(1)}, f32[1,5,5]{2,0,1:T(1,128)}, u32[]{:S(2)}) copy-start(f32[1,5,5]{2,0,1:T(1,128)} %param.11) | copy-start | bytes 304
  21.0 22.7 %all-to-all-start = ((f32[128,1,640]{2,1,0:T(1,128)}), f32[128,1,640]{2,1,0:T(1,128)S(1)}, u32[]{:S(2)}, u32[]{:S(2)}) async-start(f32[128,1,640]{2,1,0:T(1,128)} %get-tuple-element.9), calls=%async_computation | async-start | bytes 655360 | tf_op jit(solution)/shard_map/all_to_all | solution.py:355
  64.7 40.6 %copy-start.2 = (f32[1,64,64]{2,1,0:T(8,128)S(1)}, f32[1,64,64]{2,1,0:T(8,128)}, u32[]{:S(2)}) copy-start(f32[1,64,64]{2,1,0:T(8,128)} %param.14) | copy-start | bytes 49156
  111.2 36.7 %copy-start.1 = (f32[1,256,256]{2,1,0:T(8,128)S(1)}, f32[1,256,256]{2,1,0:T(8,128)}, u32[]{:S(2)}) copy-start(f32[1,256,256]{2,1,0:T(8,128)} %param.13) | copy-start | bytes 786436
